TPU v7x, 128 devices: a whole 4x4x4 slice. The times are simulated.
128 devices in a mesh: genome: 16 (over z, x), trow: 2 (over core), tcol: 4 (over y).
Axes of the slice: x: 4, y: 4, z: 4, core: 2. Of those that a mesh axis runs over, the one named last changes fastest.
Arguments:
- ldscore: float32 [16384], P('genome'), may hold values from 1 to 100
- zscores: bfloat16 [16384, 4096], P('genome', ('trow', 'tcol')), may hold values from -30 to 30
Outputs:
- rg: float32 [2, 2048, 2, 2048], P('trow', 'genome', None, 'tcol')
- rg_se: float32 [2, 2048, 2, 2048], P('trow', 'genome', None, 'tcol')
All inputs are finite; a program needn't handle non-finite values.
Results may differ from a plain program's by a relative error of at most 0.038.
Values may be sent and summed in bfloat16 or wider, within the bound.
A program may use at most 192 MiB of HBM per device.

v0:
```python
import jax
import jax.numpy as jnp
from jax import lax
from jax.sharding import PartitionSpec as P

floor_value = 0.002


def contract(left, right):
    return lax.dot_general(
        left, right, (((0,), (0,)), ((), ())), preferred_element_type=jnp.float32
    )


def slope_fit(inv_sum, ld_sum, y_sum, l_sum, count):
    return (inv_sum * l_sum - count * y_sum) / (inv_sum * ld_sum - count * count)


def weights_for(herit_pos, ld_column):
    return (1.0 / (1.0 + herit_pos[None, :] * ld_column[:, None])).astype(jnp.bfloat16)


def coupling(tiles):
    return (tiles[2] * tiles[1] - tiles[3] * tiles[0]) / (tiles[2] * tiles[4] - tiles[3] * tiles[3])


def per_device(ldscore, zscores):
    blocks = lax.axis_size("genome")
    grid_rows = lax.axis_size("trow")
    grid_cols = lax.axis_size("tcol")
    snp_count = zscores.shape[0]
    shard_width = zscores.shape[1]
    traits = shard_width * grid_rows * grid_cols
    row_width = traits // grid_rows
    row_share = row_width // blocks
    row_index = lax.axis_index("trow")
    col_index = lax.axis_index("tcol")
    genome_index = lax.axis_index("genome")
    ld_weight = 1.0 / ldscore
    z_float = zscores.astype(jnp.float32)
    z_square = z_float * z_float
    own_stats = jnp.stack(
        [jnp.sum(z_square * ld_weight[:, None], axis=0), jnp.sum(z_square, axis=0)]
    )
    own_scalars = jnp.stack([jnp.sum(ld_weight), jnp.sum(ldscore)])
    all_stats, all_scalars = (
        lax.all_gather(own_stats[None], ("genome", "trow", "tcol"), axis=0, tiled=True),
        lax.all_gather(own_scalars[None], ("genome", "trow", "tcol"), axis=0, tiled=True),
    )
    all_stats = all_stats.reshape(blocks, grid_rows * grid_cols, 2, shard_width)
    all_stats = all_stats.transpose(0, 2, 1, 3).reshape(blocks, 2, traits)
    all_scalars = all_scalars.reshape(blocks, grid_rows * grid_cols, 2)[:, 0, :]
    total_stats = jnp.sum(all_stats, axis=0)
    total_scalars = jnp.sum(all_scalars, axis=0)
    herit_full = slope_fit(
        total_scalars[0],
        total_scalars[1],
        total_stats[0],
        total_stats[1],
        float(snp_count * blocks),
    )
    rest_stats = total_stats[None] - all_stats
    rest_scalars = total_scalars[None] - all_scalars
    herit_del = slope_fit(
        rest_scalars[:, 0:1],
        rest_scalars[:, 1:2],
        rest_stats[:, 0],
        rest_stats[:, 1],
        float(snp_count * (blocks - 1)),
    )
    herit_pos = jnp.maximum(herit_full, 0.0)
    col_z = lax.all_gather(zscores, "trow", axis=1, tiled=True)
    col_herit = lax.dynamic_index_in_dim(
        herit_pos.reshape(grid_rows, grid_cols, shard_width), col_index, 1, keepdims=False
    ).reshape(-1)
    col_u = weights_for(col_herit, ldscore)
    col_zu = (col_z.astype(jnp.float32) * col_u.astype(jnp.float32)).astype(jnp.bfloat16)
    piece = lax.all_gather(zscores, "tcol", axis=1, tiled=True)
    herit_rows = lax.dynamic_slice_in_dim(herit_pos, row_index * row_width, piece.shape[1])
    row_u = weights_for(herit_rows, ldscore)
    u_float = row_u.astype(jnp.float32)
    scaled = piece.astype(jnp.float32) * u_float
    row_zu = scaled.astype(jnp.bfloat16)
    row_scaled = (scaled * ld_weight[:, None]).astype(jnp.bfloat16)
    products = [contract(row_scaled, col_zu), contract(row_zu, col_zu)]
    row_inv = (u_float * ld_weight[:, None]).astype(jnp.bfloat16)
    row_ld = (u_float * ldscore[:, None]).astype(jnp.bfloat16)
    products = products + [
        contract(row_inv, col_u),
        contract(row_u, col_u),
        contract(row_ld, col_u),
    ]
    sums = jnp.stack(products)
    sums = sums.astype(jnp.bfloat16)[:, None]
    row_start = row_index * row_width + genome_index * row_share
    tiles = lax.all_to_all(sums, "genome", split_axis=2, concat_axis=1, tiled=True)
    tile_values = tiles.astype(jnp.float32)
    totals = jnp.sum(tile_values, axis=1)
    deleted = totals[:, None] - tile_values
    full_g = coupling(totals)
    del_g = coupling(deleted)
    herit_floor = jnp.maximum(herit_full, floor_value)
    del_floor = jnp.maximum(herit_del, floor_value)
    rows_full = lax.dynamic_slice_in_dim(herit_floor, row_start, row_share)
    cols_full = lax.dynamic_index_in_dim(
        herit_floor.reshape(grid_rows, grid_cols, shard_width), col_index, 1, keepdims=False
    ).reshape(-1)
    rows_del = lax.dynamic_slice_in_dim(del_floor, row_start, row_share, axis=1)
    cols_del = lax.dynamic_index_in_dim(
        del_floor.reshape(blocks, grid_rows, grid_cols, shard_width), col_index, 2, keepdims=False
    ).reshape(blocks, -1)
    rg_tile = full_g / jnp.sqrt(rows_full[:, None] * cols_full[None, :])
    rg_del = del_g / jnp.sqrt(rows_del[:, :, None] * cols_del[:, None, :])
    mean_del = jnp.mean(rg_del, axis=0)
    differ = rg_del - mean_del[None]
    spread = jnp.sum(differ * differ, axis=0)
    se_tile = jnp.sqrt((blocks - 1) / blocks * spread)
    out_shape = (1, row_share, grid_rows, shard_width)
    return (rg_tile.reshape(out_shape), se_tile.reshape(out_shape))


def solution(mesh):
    return jax.shard_map(
        per_device,
        mesh=mesh,
        in_specs=(P("genome"), P("genome", ("trow", "tcol"))),
        out_specs=(P("trow", "genome", None, "tcol"), P("trow", "genome", None, "tcol")),
        check_vma=False,
    )
```

profile of v0, /device:TPU:17, one launch (start us, length us, event | category | flops | bytes accessed | tf_op | source)
XLA Modules:
  0.0 782.9 jit_solution(10071057856532654931)
XLA Ops:
  7.2 0.7 all-gather.8.cloned.1.call-update
  7.9 0.7 all-gather.6.cloned.1.call-update
  8.7 1.3 fusion.41
  10.0 1.5 maximum_dynamic-update-slice_fusion
  11.4 66.7 %all-reduce = f32[256]{0:T(256)S(1)} all-reduce(f32[256]{0:T(256)S(1)} %maximum_dynamic-update-slice_fusion), channel_id=2, replica_groups=mesh['genome'=16,'trow'=2,'tcol'=4] {'genome','trow','tcol'}, use_global_device_ids=true, to_apply=%add | all-reduce | flops 256 | bytes 2048
  78.1 0.1 reshape.288
  78.3 0.6 fusion.48
  80.2 1.6 multiply_reduce_fusion.1
  81.8 49.7 %all-gather.2 = f32[128,2,512]{2,1,0:T(2,128)S(1)} all-gather(f32[1,2,512]{2,1,0:T(2,128)S(1)} %maximum_bitcast_fusion), channel_id=3, replica_groups=mesh['genome'=16,'trow'=2,'tcol'=4] {'genome','trow','tcol'}, dimensions={0}, use_global_device_ids=true | all-gather | bytes 528384 | tf_op jit(solution)/shard_map/all_gather | solution.py:47
  131.6 0.7 fusion.40
  132.4 11.0 %bitcast_dynamic-update-slice_fusion.4 = bf16[5,1,2048,1024]{3,2,1,0:T(8,128)(2,1)} fusion(bf16[1024,2048]{1,0:T(8,128)(2,1)} %all-gather.6.cloned.1.call-done, f32[1024]{0:T(1024)S(1)} %get-tuple-element.19, f32[1024]{0:T(1024)} %param.2, f32[2048]{0:T(1024)S(1)} %dynamic_slice.20, bf16[1024,1024]{1,0:T(8,128)(2,1)} %all-gather.8.cloned.1.call-done, ...), kind=kOutput, calls=%fused_computation.27 | convolution fusion | flops 4324327424 | bytes 10510336 | tf_op jit(solution)/shard_map/dot_general | solution.py:10
  143.4 16.8 %bitcast_dynamic-update-slice_fusion.3 = bf16[5,1,2048,1024]{3,2,1,0:T(8,128)(2,1)} fusion(bf16[5,1,2048,1024]{3,2,1,0:T(8,128)(2,1)} %bitcast_dynamic-update-slice_fusion.4, bf16[1024,2048]{1,0:T(8,128)(2,1)S(1)} %copy-done.1, f32[1024]{0:T(1024)S(1)} %copy-done, f32[2048]{0:T(1024)S(1)} %dynamic_slice.20, bf16[1024,1024]{1,0:T(8,128)(2,1)S(1)} %copy-done.2, ...), kind=kOutput, calls=%fused_computation.26 | convolution fusion | flops 4322230272 | bytes 10506240 | tf_op jit(solution)/shard_map/dot_general | solution.py:10
  160.2 7.2 bitcast_dynamic-update-slice_fusion.2
  167.3 6.9 bitcast_dynamic-update-slice_fusion.1
  174.2 6.9 bitcast_dynamic-update-slice_fusion
  181.1 23.9 %copy.19 = bf16[5,1,2048,1024]{3,0,1,2:T(8,128)(2,1)} copy(bf16[5,1,2048,1024]{3,2,1,0:T(8,128)(2,1)} %bitcast_dynamic-update-slice_fusion) | data formatting | bytes 41943040 | tf_op jit(solution)/shard_map/stack | solution.py:93
  205.0 6.1 all-to-all-start
  211.2 0.1 copy.31
  211.7 0.2 mul.285
  211.9 0.2 squeeze.18
  212.1 0.4 maximum_reduce_fusion
  212.7 493.6 %all-to-all-done = bf16[5,1,2048,1024]{3,0,1,2:T(8,128)(2,1)} async-done(((bf16[5,1,2048,1024]{3,0,1,2:T(8,128)(2,1)}), bf16[5,1,2048,1024]{3,0,1,2:T(8,128)(2,1)}, u32[]{:S(2)}, u32[]{:S(2)}) %all-to-all-start) | async-done | bytes 20971552 | tf_op jit(solution)/shard_map/all_to_all | solution.py:96
  706.3 23.2 %copy.20 = bf16[5,1,2048,1024]{3,2,0,1:T(8,128)(2,1)S(1)} copy(bf16[5,1,2048,1024]{3,0,1,2:T(8,128)(2,1)} %all-to-all-done) | data formatting | bytes 41943040 | tf_op jit(solution)/shard_map/all_to_all | solution.py:96
  729.5 4.3 convert_reduce_fusion
  733.8 0.3 fusion.27
  734.1 14.2 %convert_subtract_fusion = f32[5,16,128,1024]{3,2,1,0:T(8,128)} fusion(bf16[5,16,128,1024]{3,2,1,0:T(8,128)(2,1)S(1)} %bitcast.64, f32[5,128,1024]{2,1,0:T(8,128)S(1)} %convert_reduce_fusion), kind=kLoop, calls=%fused_computation | loop fusion | flops 20971520 | bytes 65536000 | tf_op jit(solution)/shard_map/sub | solution.py:99
  748.4 0.4 div.75
  748.8 19.8 %fusion.44 = (f32[128,1024]{1,0:T(8,128)S(1)}, f32[16,128,1024]{2,1,0:T(8,128)}) fusion(f32[16,1024]{1,0:T(8,128)S(1)} %bitcast.69, f32[16,128]{1,0:T(8,128)S(1)} %fusion.33, f32[5,16,128,1024]{3,2,1,0:T(8,128)} %convert_subtract_fusion), kind=kLoop, calls=%fused_computation.84 | loop fusion | flops 20840448 | bytes 50929664 | tf_op jit(solution)/shard_map/reduce_sum | solution.py:114
  768.6 4.6 multiply_reduce_fusion
  773.2 0.1 multiply_sqrt_fusion
  773.4 1.2 sqrt.22
  774.6 1.1 rsqrt_multiply_fusion
  (34 shorter events, 0.9 us)
Async XLA Ops:
  7.2 125.2 %all-gather.8.cloned.1.call-start = ((), (), s32[]{:S(2)}) async-start(), calls=%async_computation.2 | async-start | bytes 3145728 | tf_op jit(solution)/shard_map/all_gather | solution.py:72
  7.9 124.4 %all-gather.6.cloned.1.call-start = ((), (), s32[]{:S(2)}) async-start(), calls=%async_computation.1 | async-start | bytes 5242880 | tf_op jit(solution)/shard_map/all_gather | solution.py:78
  132.4 11.0 %copy-start = (f32[1024]{0:T(1024)S(1)}, f32[1024]{0:T(1024)}, u32[]{:S(2)}) copy-start(f32[1024]{0:T(1024)} %param.2) | copy-start | bytes 12292
  132.4 11.0 %copy-start.1 = (bf16[1024,2048]{1,0:T(8,128)(2,1)S(1)}, bf16[1024,2048]{1,0:T(8,128)(2,1)}, u32[]{:S(2)}) copy-start(bf16[1024,2048]{1,0:T(8,128)(2,1)} %all-gather.6.cloned.1.call-done) | copy-start | bytes 12582916
  132.4 11.0 %copy-start.2 = (bf16[1024,1024]{1,0:T(8,128)(2,1)S(1)}, bf16[1024,1024]{1,0:T(8,128)(2,1)}, u32[]{:S(2)}) copy-start(bf16[1024,1024]{1,0:T(8,128)(2,1)} %all-gather.8.cloned.1.call-done) | copy-start | bytes 6291460
  205.0 501.2 %all-to-all-start = ((bf16[5,1,2048,1024]{3,0,1,2:T(8,128)(2,1)}), bf16[5,1,2048,1024]{3,0,1,2:T(8,128)(2,1)}, u32[]{:S(2)}, u32[]{:S(2)}) async-start(bf16[5,1,2048,1024]{3,0,1,2:T(8,128)(2,1)} %copy.19), calls=%async_computation | async-start | bytes 67108864 | tf_op jit(solution)/shard_map/all_to_all | solution.py:96
Sparse Core Ops, SparseCore 0:
  9.6 16.0 all-gather.7
  27.4 48.9 all-gather.5
where the time goes:
time: 797 us; the launch traced here: 783 us
  waiting for transfers between devices  495 us (62%)
  blocking collectives  116 us (15%)
  local copies, waits for them, and re-layouts  50.4 us (6%)
  other arithmetic  50.3 us (6%)
  matrix products  48.7 us (6%)
  between operations  16 us (2%)
    all_to_all x1, waiting for transfers between devices, per_device(): lax.all_to_all(sums, 'genome', split_axis=2, concat_axis=1, tiled=True)  494 us
    unnamed x1, blocking collectives  66.7 us
    all_gather x1, blocking collectives, per_device(): lax.all_gather(own_stats[None], ('genome', 'trow', 'tcol'), axis=0, tiled...  49.7 us
    dot_general x5, matrix products, contract(): lax.dot_general(left, right, (((0,), (0,)), ((), ())), preferred_element_...  48.7 us
    another operation x1, local copies, waits for them, and re-layouts, per_device(): sums = jnp.stack(products)  23.9 us
    all_to_all x1, local copies, waits for them, and re-layouts, per_device(): lax.all_to_all(sums, 'genome', split_axis=2, concat_axis=1, tiled=True)  23.2 us
    reduce_sum x1, other arithmetic, per_device(): mean_del = jnp.mean(rg_del, axis=0)  19.8 us
  transfers between devices with their start and end apart: 3, of which 1 were waited for; matrix products, arithmetic and copies ran while one was open for 1% of the time, Pallas kernels for 0%

commit v1 on v0

v1 whole, which is shorter than its diff:
```python
import functools

import jax
import jax.numpy as jnp
from jax import lax
from jax.experimental import pallas as pl
from jax.experimental.pallas import tpu as pltpu
from jax.sharding import PartitionSpec as P

floor_value = 0.002
MESH = pl.DeviceIdType.MESH
f32 = jnp.float32
bf16 = jnp.bfloat16

SNP = 1024
TB = 512
LANE = 128
NCH = SNP // LANE
NB = 16
NQ = 4
NX = 4
ROWS = 128
HALF = 256

R_FULL = NB
R_POS = NB + 1
TROWS = 24


def recip(value):
    return 1.0 / value


def column_tile(tile):
    return jnp.transpose(jnp.concatenate([tile] * (LANE // 8), axis=0))


def kernel(
    ld_ref,
    z_ref,
    rg_ref,
    se_ref,
    stage,
    allst,
    ldcol,
    lwcol,
    hrow,
    hdq,
    hdr,
    hdt,
    hcols,
    rbuf,
    cbuf,
    colw,
    lhsy,
    sendy,
    sendx,
    recvy,
    recvx,
    lhsw,
    ucol,
    wbuf,
    wext,
    wfull,
    wfext,
    msend,
    mrecv,
    y_send,
    y_recv,
    g_send,
    g_recv,
    c_send,
    c_recv,
    r_send,
    r_recv,
    a_send,
    a_recv,
    e_send,
    e_recv,
    m_send,
    m_recv,
):
    g = lax.axis_index("genome")
    r = lax.axis_index("trow")
    y = lax.axis_index("tcol")
    zz = g // NX
    x = g % NX
    other = 1 - r
    diag = zz == y
    own_cb = jnp.where(zz > y, other, r)
    half = (x // 2 + r) % 2

    barrier = pltpu.get_barrier_semaphore()

    def greet(dev):
        pl.semaphore_signal(barrier, inc=1, device_id=dev, device_id_type=MESH)

    @pl.loop(1, NB)
    def _(k):
        greet(((g + k) % NB, r, y))

    @pl.loop(1, NQ)
    def _(k):
        greet((g, r, (y + k) % NQ))

    greet((g, other, y))

    @pl.when(diag)
    def _():
        @pl.loop(0, NX)
        def _(k):
            greet((zz * NX + k, other, y))

    @pl.when(jnp.logical_not(diag))
    def _():
        @pl.loop(0, NX)
        def _(k):
            greet((y * NX + k, r, zz))
            greet((y * NX + k, other, zz))

    ld_tile = ld_ref[...]
    ld_t = column_tile(ld_tile)
    for c in range(NCH):
        col = jnp.broadcast_to(ld_t[:, c : c + 1], (LANE, LANE))
        ldcol[c * LANE : (c + 1) * LANE, :] = col
        lwcol[c * LANE : (c + 1) * LANE, :] = recip(col)
    for c in range(TB // LANE):
        lanes = slice(c * LANE, (c + 1) * LANE)
        acc_y = jnp.zeros((8, LANE), f32)
        acc_l = jnp.zeros((8, LANE), f32)
        for s in range(NCH):
            rows = slice(s * LANE, (s + 1) * LANE)
            zraw = z_ref[rows, lanes]
            rbuf[y, c, rows, :] = zraw
            zc = zraw.astype(f32)
            sq = zc * zc
            acc_l = acc_l + jnp.sum(sq.reshape(LANE // 8, 8, LANE), axis=0)
            acc_y = acc_y + jnp.sum((sq * lwcol[rows, :]).reshape(LANE // 8, 8, LANE), axis=0)
        stage[y, c : c + 1, :] = jnp.sum(acc_y, axis=0, keepdims=True)
        stage[y, 4 + c : 5 + c, :] = jnp.sum(acc_l, axis=0, keepdims=True)
    stage[NQ] = ld_tile

    @pl.when(diag)
    def _():
        pl.semaphore_wait(barrier, NB - 1 + NQ - 1 + 1 + NX)

    @pl.when(jnp.logical_not(diag))
    def _():
        pl.semaphore_wait(barrier, NB - 1 + NQ - 1 + 1 + 2 * NX)

    def y_copy(k):
        return pltpu.make_async_remote_copy(
            src_ref=stage.at[y],
            dst_ref=stage.at[y],
            send_sem=y_send.at[k],
            recv_sem=y_recv.at[y],
            device_id=(g, r, (y + k) % NQ),
            device_id_type=MESH,
        )

    @pl.loop(1, NQ)
    def _(k):
        y_copy(k).start()

    def core_copy(src, dst, i):
        return pltpu.make_async_remote_copy(
            src_ref=src,
            dst_ref=dst,
            send_sem=c_send.at[i],
            recv_sem=c_recv.at[i],
            device_id=(g, other, y),
            device_id_type=MESH,
        )

    core_copy(z_ref, cbuf, 0).start()

    def chunk_of(step):
        return (x + 3 * step + 2) % NX

    def row_copy(k, c):
        return pltpu.make_async_remote_copy(
            src_ref=rbuf.at[y, c],
            dst_ref=rbuf.at[y, c],
            send_sem=r_send.at[k, c],
            recv_sem=r_recv.at[y, c],
            device_id=(g, r, (y + k) % NQ),
            device_id_type=MESH,
        )

    @pl.loop(0, NX)
    def _(step):
        @pl.loop(1, NQ)
        def _(k):
            row_copy(k, chunk_of(step)).start()

    @pl.loop(1, NQ)
    def _(k):
        q = (y + k) % NQ
        pltpu.make_async_copy(stage.at[q], stage.at[q], y_recv.at[q]).wait()

    def g_copy(k):
        return pltpu.make_async_remote_copy(
            src_ref=stage,
            dst_ref=allst.at[g],
            send_sem=g_send.at[k],
            recv_sem=g_recv.at[g],
            device_id=((g + k) % NB, r, y),
            device_id_type=MESH,
        )

    @pl.loop(1, NB)
    def _(k):
        g_copy(k).start()

    allst[g] = stage[...]

    @pl.loop(1, NB)
    def _(k):
        b = (g + k) % NB
        pltpu.make_async_copy(allst.at[b], allst.at[b], g_recv.at[b]).wait()

    inv_b = []
    lds_b = []
    for b in range(NB):
        tile = allst[b, NQ]
        inv_b.append(jnp.sum(jnp.sum(recip(tile), axis=0, keepdims=True), axis=1, keepdims=True))
        lds_b.append(jnp.sum(jnp.sum(tile, axis=0, keepdims=True), axis=1, keepdims=True))
    inv_t = functools.reduce(jnp.add, inv_b)
    lds_t = functools.reduce(jnp.add, lds_b)

    def slope(inv, ld, sums, count):
        return (inv * sums[4:8] - count * sums[0:4]) / (inv * ld - count * count)

    n_full = float(SNP * NB)
    n_del = float(SNP * (NB - 1))

    def total_of(q):
        total = allst[0, q]
        for b in range(1, NB):
            total = total + allst[b, q]
        return total

    for q in range(NQ):
        h = jnp.maximum(slope(inv_t, lds_t, total_of(q), n_full), 0.0)
        for c in range(NX):
            hrow[q * NX + c] = h[c : c + 1, :]

    def scaled(h):
        return lax.rsqrt(jnp.maximum(h, floor_value))

    tot_c = total_of(y)
    h_full = slope(inv_t, lds_t, tot_c, n_full)
    hcols[r, TROWS - 8 : TROWS, :] = jnp.zeros((8, TB), f32)
    for c in range(NX):
        lanes = slice(c * LANE, (c + 1) * LANE)
        hcols[r, R_FULL : R_FULL + 1, lanes] = scaled(h_full[c : c + 1, :])
        hcols[r, R_POS : R_POS + 1, lanes] = jnp.maximum(h_full[c : c + 1, :], 0.0)
    for b in range(NB):
        h = scaled(slope(inv_t - inv_b[b], lds_t - lds_b[b], tot_c - allst[b, y], n_del))
        for c in range(NX):
            hcols[r, b : b + 1, c * LANE : (c + 1) * LANE] = h[c : c + 1, :]
    core_copy(hcols.at[r], hcols.at[r], 1).start()

    tot_r = total_of(zz)
    h_full = slope(inv_t, lds_t, tot_r, n_full)
    for c in range(NX):
        hdq[R_FULL, c] = scaled(h_full[c : c + 1, :])
        hdq[R_POS, c] = jnp.maximum(h_full[c : c + 1, :], 0.0)
    for b in range(NB):
        h = scaled(slope(inv_t - inv_b[b], lds_t - lds_b[b], tot_r - allst[b, zz], n_del))
        for c in range(NX):
            hdq[b, c] = h[c : c + 1, :]
    hdr[...] = jnp.zeros((LANE, LANE), f32)
    for b in range(R_POS + 1):
        hdr[b : b + 1, :] = hdq[b, x]
    hdt[...] = jnp.transpose(hdr[...])

    def weigh_columns(src, cb):
        @pl.loop(0, NCH)
        def _(s):
            rows = pl.ds(pl.multiple_of(s * LANE, LANE), LANE)
            for c in range(TB // LANE):
                lanes = slice(c * LANE, (c + 1) * LANE)
                h = hcols[cb, R_POS : R_POS + 1, lanes]
                u = recip(1.0 + h * ldcol[rows, :]).astype(bf16).astype(f32)
                colw[cb, rows, lanes] = (src[rows, lanes].astype(f32) * u).astype(bf16)

    weigh_columns(z_ref, r)
    pltpu.make_async_copy(hcols.at[other], hcols.at[other], c_recv.at[1]).wait()
    pltpu.make_async_copy(cbuf, cbuf, c_recv.at[0]).wait()
    weigh_columns(cbuf, other)

    def pair_copy(q, c):
        return pltpu.make_async_remote_copy(
            src_ref=sendy.at[q * NX + c],
            dst_ref=recvy.at[g],
            send_sem=a_send.at[q * NX + c],
            recv_sem=a_recv.at[g],
            device_id=(q * NX + c, r, y),
            device_id_type=MESH,
        )

    def extra_copy(c):
        return pltpu.make_async_remote_copy(
            src_ref=sendx.at[c],
            dst_ref=recvx.at[g],
            send_sem=e_send.at[c],
            recv_sem=e_recv.at[g],
            device_id=(y * NX + c, r, y),
            device_id_type=MESH,
        )

    def contract(left, right):
        return lax.dot_general(left, right, (((0,), (0,)), ((), ())), preferred_element_type=f32)

    def pair_sums(q, c):
        h = hrow[q * NX + c]
        for s in range(NCH):
            rows = slice(s * LANE, (s + 1) * LANE)
            u = recip(1.0 + h * ldcol[rows, :]).astype(bf16).astype(f32)
            value = rbuf[q, c, rows, :].astype(f32) * u
            lhsy[rows, 0:LANE] = (value * lwcol[rows, :]).astype(bf16)
            lhsy[rows, LANE : 2 * LANE] = value.astype(bf16)
        cb = jnp.where(q > y, other, r)
        sums = contract(lhsy[...], colw[cb]).astype(bf16)
        mine = q * NX + c == g

        @pl.when(mine)
        def _():
            recvy[g, 0] = sums[0:ROWS]
            recvy[g, 1] = sums[ROWS : 2 * ROWS]

        @pl.when(jnp.logical_not(mine))
        def _():
            sendy[q * NX + c, 0] = sums[0:ROWS]
            sendy[q * NX + c, 1] = sums[ROWS : 2 * ROWS]
            pair_copy(q, c).start()

        @pl.when(q == y)
        def _():
            side = (c // 2 + r) % 2
            lanes = pl.ds(pl.multiple_of(side * HALF, HALF), HALF)
            extra = contract(lhsy[...], colw[other, :, lanes]).astype(bf16)

            @pl.when(mine)
            def _():
                recvx[g, 0] = extra[0:ROWS]
                recvx[g, 1] = extra[ROWS : 2 * ROWS]

            @pl.when(jnp.logical_not(mine))
            def _():
                sendx[c, 0] = extra[0:ROWS]
                sendx[c, 1] = extra[ROWS : 2 * ROWS]
                extra_copy(c).start()

    def weight_sums(b):
        tile = allst[b, NQ]
        inv = recip(tile)
        h = hdt[:, R_POS : R_POS + 1]
        for c in range(NCH):
            lanes = slice(c * LANE, (c + 1) * LANE)
            row = tile[c : c + 1, :]
            u16 = recip(1.0 + h * row).astype(bf16)
            u = u16.astype(f32)
            lhsw[0:ROWS, lanes] = (u * inv[c : c + 1, :]).astype(bf16)
            lhsw[ROWS : 2 * ROWS, lanes] = u16
            lhsw[2 * ROWS : 3 * ROWS, lanes] = (u * row).astype(bf16)
        ldc = column_tile(tile)
        h = hcols[own_cb, R_POS : R_POS + 1, :]
        for c in range(NCH):
            ucol[c * LANE : (c + 1) * LANE, :] = recip(1.0 + ldc[:, c : c + 1] * h).astype(bf16)
        wbuf[b] = jnp.dot(lhsw[...], ucol[...], preferred_element_type=f32)

        @pl.when(diag)
        def _():
            lanes = pl.ds(pl.multiple_of(half * HALF, HALF), HALF)
            h = hcols[other, R_POS : R_POS + 1, lanes]
            for c in range(NCH):
                ucol[c * LANE : (c + 1) * LANE, 0:HALF] = recip(1.0 + ldc[:, c : c + 1] * h).astype(
                    bf16
                )
            wext[b] = jnp.dot(lhsw[...], ucol[:, 0:HALF], preferred_element_type=f32)

    @pl.loop(0, NX)
    def _(step):
        c = chunk_of(step)

        @pl.loop(0, NQ)
        def _(k):
            q = (zz + k) % NQ

            @pl.when(q != y)
            def _():
                pltpu.make_async_copy(rbuf.at[q, c], rbuf.at[q, c], r_recv.at[q, c]).wait()

            pair_sums(q, c)

        @pl.loop(0, NB // NX)
        def _(k):
            weight_sums(step * (NB // NX) + k)

    def factors(weights, full, cols, width):
        @pl.loop(0, ROWS // 8)
        def _(t):
            base = pl.multiple_of(t * 8, 8)

            def at(i):
                return pl.ds(i * ROWS + base, 8)

            for c in range(width // LANE):
                lanes = slice(c * LANE, (c + 1) * LANE)
                tot = [weights[0, at(i), lanes] for i in range(3)]
                for b in range(1, NB):
                    tot = [tot[i] + weights[b, at(i), lanes] for i in range(3)]

                def pair(w, b):
                    scale = hdt[pl.ds(base, 8), b : b + 1] * cols(b, c)
                    k = scale / (w[0] * w[2] - w[1] * w[1])
                    return w[0] * k, w[1] * k

                full[0, pl.ds(base, 8), lanes], full[1, pl.ds(base, 8), lanes] = pair(tot, R_FULL)
                for b in range(NB):
                    w = [tot[i] - weights[b, at(i), lanes] for i in range(3)]
                    weights[b, at(0), lanes], weights[b, at(1), lanes] = pair(w, b)

    def own_cols(b, c):
        return hcols[own_cb, b : b + 1, c * LANE : (c + 1) * LANE]

    def extra_cols(b, c):
        lanes = pl.ds(pl.multiple_of(half * HALF + c * LANE, LANE), LANE)
        return hcols[other, b : b + 1, lanes]

    factors(wbuf, wfull, own_cols, TB)

    @pl.when(diag)
    def _():
        factors(wext, wfext, extra_cols, HALF)

    def finish(pairs, weights, full, cb, start, width):
        @pl.loop(0, ROWS // 16)
        def _(t):
            base = pl.multiple_of(t * 16, 16)
            rows = pl.ds(base, 16)
            for c in range(width // LANE):
                lanes = slice(c * LANE, (c + 1) * LANE)
                tot0 = pairs[0, 0, rows, lanes].astype(f32)
                tot1 = pairs[0, 1, rows, lanes].astype(f32)
                for b in range(1, NB):
                    tot0 = tot0 + pairs[b, 0, rows, lanes].astype(f32)
                    tot1 = tot1 + pairs[b, 1, rows, lanes].astype(f32)
                out = pl.ds(pl.multiple_of(start + c * LANE, LANE), LANE)
                rg_ref[cb, rows, out] = full[0, rows, lanes] * tot1 - full[1, rows, lanes] * tot0
                values = []
                for b in range(NB):
                    del0 = tot0 - pairs[b, 0, rows, lanes].astype(f32)
                    del1 = tot1 - pairs[b, 1, rows, lanes].astype(f32)
                    values.append(
                        weights[b, pl.ds(base, 16), lanes] * del1
                        - weights[b, pl.ds(ROWS + base, 16), lanes] * del0
                    )
                mean = functools.reduce(jnp.add, values) * (1.0 / NB)
                spread = functools.reduce(jnp.add, [(v - mean) * (v - mean) for v in values])
                se_ref[cb, rows, out] = jnp.sqrt((NB - 1) / NB * spread)

    @pl.loop(1, NB)
    def _(k):
        b = (g + k) % NB
        pltpu.make_async_copy(recvy.at[b], recvy.at[b], a_recv.at[b]).wait()

    finish(recvy, wbuf, wfull, own_cb, 0, TB)

    @pl.when(diag)
    def _():
        @pl.loop(1, NB)
        def _(k):
            b = (g + k) % NB
            pltpu.make_async_copy(recvx.at[b], recvx.at[b], e_recv.at[b]).wait()

        finish(recvx, wext, wfext, other, half * HALF, HALF)

    def mirror_copy(k):
        dev = (
            jnp.where(diag, zz * NX + k, y * NX + k),
            jnp.where(diag, other, own_cb),
            zz,
        )
        return pltpu.make_async_remote_copy(
            src_ref=msend.at[k],
            dst_ref=mrecv.at[x],
            send_sem=m_send.at[k],
            recv_sem=m_recv.at[x],
            device_id=dev,
            device_id_type=MESH,
        )

    send_first = jnp.where(diag, 2 * half, 0)
    recv_first = jnp.where(diag, 2 * (1 - half), 0)
    pieces = jnp.where(diag, 2, NX)
    send_cb = jnp.where(diag, other, own_cb)
    recv_cb = jnp.where(diag, other, 1 - own_cb)

    @pl.loop(0, pieces)
    def _(i):
        k = send_first + i
        lanes = pl.ds(pl.multiple_of(k * LANE, LANE), LANE)
        msend[k, 0] = jnp.transpose(rg_ref[send_cb, :, lanes]).astype(bf16)
        msend[k, 1] = jnp.transpose(se_ref[send_cb, :, lanes]).astype(bf16)
        mirror_copy(k).start()

    @pl.loop(0, pieces)
    def _(i):
        k = recv_first + i
        lanes = pl.ds(pl.multiple_of(k * LANE, LANE), LANE)
        pltpu.make_async_copy(mrecv.at[k], mrecv.at[k], m_recv.at[k]).wait()
        rg_ref[recv_cb, :, lanes] = mrecv[k, 0].astype(f32)
        se_ref[recv_cb, :, lanes] = mrecv[k, 1].astype(f32)

    @pl.loop(1, NQ)
    def _(k):
        y_copy(k).wait_send()

        @pl.loop(0, NX)
        def _(c):
            row_copy(k, c).wait_send()

    core_copy(z_ref, cbuf, 0).wait_send()
    core_copy(hcols.at[r], hcols.at[r], 1).wait_send()

    @pl.loop(1, NB)
    def _(k):
        g_copy(k).wait_send()
        p = (g + k) % NB
        pair_copy(p // NX, p % NX).wait_send()

    @pl.loop(0, NX)
    def _(c):
        @pl.when(y * NX + c != g)
        def _():
            extra_copy(c).wait_send()

    @pl.loop(0, pieces)
    def _(i):
        mirror_copy(send_first + i).wait_send()


def per_device(ldscore, zscores):
    dma = pltpu.SemaphoreType.DMA
    out = jax.ShapeDtypeStruct((2, ROWS, TB), f32)
    rg, se = pl.pallas_call(
        kernel,
        out_shape=(out, out),
        in_specs=[pl.BlockSpec(memory_space=pltpu.VMEM)] * 2,
        out_specs=[pl.BlockSpec(memory_space=pltpu.VMEM)] * 2,
        scratch_shapes=[
            pltpu.VMEM((NQ + 1, 8, LANE), f32),
            pltpu.VMEM((NB, NQ + 1, 8, LANE), f32),
            pltpu.VMEM((SNP, LANE), f32),
            pltpu.VMEM((SNP, LANE), f32),
            pltpu.VMEM((NQ * NX, 1, LANE), f32),
            pltpu.VMEM((R_POS + 1, NX, 1, LANE), f32),
            pltpu.VMEM((LANE, LANE), f32),
            pltpu.VMEM((LANE, LANE), f32),
            pltpu.VMEM((2, TROWS, TB), f32),
            pltpu.VMEM((NQ, NX, SNP, LANE), bf16),
            pltpu.VMEM((SNP, TB), bf16),
            pltpu.VMEM((2, SNP, TB), bf16),
            pltpu.VMEM((SNP, 2 * LANE), bf16),
            pltpu.VMEM((NB, 2, ROWS, TB), bf16),
            pltpu.VMEM((NX, 2, ROWS, HALF), bf16),
            pltpu.VMEM((NB, 2, ROWS, TB), bf16),
            pltpu.VMEM((NB, 2, ROWS, HALF), bf16),
            pltpu.VMEM((3 * ROWS, SNP), bf16),
            pltpu.VMEM((SNP, TB), bf16),
            pltpu.VMEM((NB, 3 * ROWS, TB), f32),
            pltpu.VMEM((NB, 3 * ROWS, HALF), f32),
            pltpu.VMEM((2, ROWS, TB), f32),
            pltpu.VMEM((2, ROWS, HALF), f32),
            pltpu.VMEM((NX, 2, LANE, LANE), bf16),
            pltpu.VMEM((NX, 2, LANE, LANE), bf16),
            dma((NQ,)),
            dma((NQ,)),
            dma((NB,)),
            dma((NB,)),
            dma((2,)),
            dma((2,)),
            dma((NQ, NX)),
            dma((NQ, NX)),
            dma((NB,)),
            dma((NB,)),
            dma((NX,)),
            dma((NB,)),
            dma((NX,)),
            dma((NX,)),
        ],
        compiler_params=pltpu.CompilerParams(
            collective_id=0, has_side_effects=True, vmem_limit_bytes=56 * 1024 * 1024
        ),
    )(ldscore.reshape(8, LANE), zscores)
    return (rg.transpose(1, 0, 2)[None], se.transpose(1, 0, 2)[None])


def solution(mesh):
    return jax.shard_map(
        per_device,
        mesh=mesh,
        in_specs=(P("genome"), P("genome", ("trow", "tcol"))),
        out_specs=(P("trow", "genome", None, "tcol"), P("trow", "genome", None, "tcol")),
        check_vma=False,
    )
```

time: 797 us -> 127 us (0.16)
  the two profiles are of different devices: /device:TPU:17 before, /device:TPU:102 now
where the time goes in v1:
time: 127 us; the launch traced here: 126 us
  Pallas kernels  122 us (96%)
  local copies, waits for them, and re-layouts  3.5 us (3%)
    pallas_call x1, Pallas kernels, per_device(): pl.pallas_call(kernel, out_shape=(out, out), in_specs=[pl.BlockSpec(memor...  122 us
    unnamed x4, local copies, waits for them, and re-layouts  3.5 us

profile of v1, /device:TPU:102, one launch (start us, length us, event | category | flops | bytes accessed | tf_op | source)
XLA Modules:
  0.0 126.4 jit_solution(10502223310120402376)
XLA Ops:
  0.6 122.3 %shard_map.41 = (f32[2,128,512]{2,1,0:T(8,128)}, f32[2,128,512]{2,1,0:T(8,128)}) custom-call(f32[8,128]{1,0:T(8,128)} %bitcast.9, bf16[1024,512]{1,0:T(8,128)(2,1)} %z_ref.1), custom_call_target="tpu_custom_call" | custom-call | tf_op jit(solution)/shard_map/pallas_call | solution.py:549
  122.9 0.0 copy-start
  122.9 2.3 %copy.4 = f32[1,128,2,512]{3,2,1,0:T(2,128)} copy(f32[1,128,2,512]{3,1,2,0:T(8,128)} %bitcast.8) | data formatting | bytes 1048576
  125.2 0.0 copy-done
  125.2 1.2 copy.5
Async XLA Ops:
  122.9 2.3 %copy-start = (f32[2,128,512]{2,1,0:T(8,128)S(1)}, f32[2,128,512]{2,1,0:T(8,128)}, u32[]{:S(2)}) copy-start(f32[2,128,512]{2,1,0:T(8,128)} %get-tuple-element.5) | copy-start | bytes 1572868

commit v2 on v1

v2 whole, which is shorter than its diff:
```python
import functools

import jax
import jax.numpy as jnp
from jax import lax
from jax.experimental import pallas as pl
from jax.experimental.pallas import tpu as pltpu
from jax.sharding import PartitionSpec as P

floor_value = 0.002
MESH = pl.DeviceIdType.MESH
f32 = jnp.float32
bf16 = jnp.bfloat16

SNP = 1024
TB = 512
LANE = 128
NCH = SNP // LANE
NB = 16
NQ = 4
NX = 4
ROWS = 128
HALF = 256

R_FULL = NB
R_POS = NB + 1
TROWS = 24

T_OTHER = NQ
T_LD = NQ + 1


def recip(value):
    return 1.0 / value


def column_tile(tile):
    return jnp.transpose(jnp.concatenate([tile] * (LANE // 8), axis=0))


def kernel(
    ld_ref,
    z_ref,
    rg_ref,
    se_ref,
    stage,
    allst,
    ldcol,
    lwcol,
    hrow,
    hdq,
    hdr,
    hdt,
    hcols,
    ctab,
    rbuf,
    cbuf,
    colw,
    lhsy,
    sendy,
    sendx,
    recvy,
    recvx,
    lhsw,
    ucol,
    wbuf,
    wext,
    wfull,
    wfext,
    msend,
    mrecv,
    y_send,
    y_recv,
    g_send,
    g_recv,
    c_send,
    c_recv,
    r_send,
    r_recv,
    f_send,
    f_recv,
    a_send,
    a_recv,
    e_send,
    e_recv,
    m_send,
    m_recv,
):
    g = lax.axis_index("genome")
    r = lax.axis_index("trow")
    y = lax.axis_index("tcol")
    zz = g // NX
    x = g % NX
    other = 1 - r
    diag = zz == y
    own_cb = jnp.where(zz > y, other, r)
    half = (x // 2 + r) % 2
    fifth = jnp.logical_and(diag, x < 2)

    barrier = pltpu.get_barrier_semaphore()

    def greet(dev):
        pl.semaphore_signal(barrier, inc=1, device_id=dev, device_id_type=MESH)

    @pl.loop(1, NB)
    def _(k):
        greet(((g + k) % NB, r, y))

    @pl.loop(1, NQ)
    def _(k):
        greet((g, r, (y + k) % NQ))

    greet((g, other, y))

    @pl.when(diag)
    def _():
        @pl.loop(0, NX)
        def _(k):
            greet((zz * NX + k, other, y))

    @pl.when(jnp.logical_not(diag))
    def _():
        @pl.loop(0, NX)
        def _(k):
            greet((y * NX + k, r, zz))
            greet((y * NX + k, other, zz))

    ld_tile = ld_ref[...]
    ld_t = column_tile(ld_tile)
    for c in range(NCH):
        col = jnp.broadcast_to(ld_t[:, c : c + 1], (LANE, LANE))
        ldcol[c * LANE : (c + 1) * LANE, :] = col
        lwcol[c * LANE : (c + 1) * LANE, :] = recip(col)
    for c in range(TB // LANE):
        lanes = slice(c * LANE, (c + 1) * LANE)
        acc_y = jnp.zeros((8, LANE), f32)
        acc_l = jnp.zeros((8, LANE), f32)
        for s in range(NCH):
            rows = slice(s * LANE, (s + 1) * LANE)
            zraw = z_ref[rows, lanes]
            rbuf[y, c, rows, :] = zraw
            zc = zraw.astype(f32)
            sq = zc * zc
            acc_l = acc_l + jnp.sum(sq.reshape(LANE // 8, 8, LANE), axis=0)
            acc_y = acc_y + jnp.sum((sq * lwcol[rows, :]).reshape(LANE // 8, 8, LANE), axis=0)
        stage[y, c : c + 1, :] = jnp.sum(acc_y, axis=0, keepdims=True)
        stage[y, 4 + c : 5 + c, :] = jnp.sum(acc_l, axis=0, keepdims=True)
    stage[T_LD] = ld_tile

    @pl.when(diag)
    def _():
        pl.semaphore_wait(barrier, NB - 1 + NQ - 1 + 1 + NX)

    @pl.when(jnp.logical_not(diag))
    def _():
        pl.semaphore_wait(barrier, NB - 1 + NQ - 1 + 1 + 2 * NX)

    def y_copy(k):
        return pltpu.make_async_remote_copy(
            src_ref=stage.at[y],
            dst_ref=stage.at[y],
            send_sem=y_send.at[k],
            recv_sem=y_recv.at[y],
            device_id=(g, r, (y + k) % NQ),
            device_id_type=MESH,
        )

    def core_copy(src, dst, i):
        return pltpu.make_async_remote_copy(
            src_ref=src,
            dst_ref=dst,
            send_sem=c_send.at[i],
            recv_sem=c_recv.at[i],
            device_id=(g, other, y),
            device_id_type=MESH,
        )

    @pl.loop(1, NQ)
    def _(k):
        y_copy(k).start()

    core_copy(stage.at[y], stage.at[T_OTHER], 0).start()
    core_copy(z_ref, cbuf, 1).start()

    def chunk_of(step):
        return (x + 3 * step + 2) % NX

    def row_copy(way, c):
        return pltpu.make_async_remote_copy(
            src_ref=rbuf.at[y, c],
            dst_ref=rbuf.at[y, c],
            send_sem=r_send.at[way, c],
            recv_sem=r_recv.at[way, c],
            device_id=(g, r, (y + 1 + 2 * way) % NQ),
            device_id_type=MESH,
        )

    def far_copy(way, c):
        q = (y + 3 + 2 * way) % NQ
        part = rbuf.at[q, c, pl.ds(pl.multiple_of(way * (SNP // 2), SNP // 2), SNP // 2)]
        return pltpu.make_async_remote_copy(
            src_ref=part,
            dst_ref=part,
            send_sem=f_send.at[way, c],
            recv_sem=f_recv.at[way, c],
            device_id=(g, r, (y + 1 + 2 * way) % NQ),
            device_id_type=MESH,
        )

    def send_chunk(step):
        c = chunk_of(step)
        row_copy(0, c).start()
        row_copy(1, c).start()

    def pass_on(step):
        c = chunk_of(step)
        for way in range(2):
            q = (y + 3 + 2 * way) % NQ
            pltpu.make_async_copy(rbuf.at[q, c], rbuf.at[q, c], r_recv.at[way, c]).wait()
            far_copy(way, c).start()

    send_chunk(0)
    send_chunk(1)

    @pl.loop(1, NQ)
    def _(k):
        q = (y + k) % NQ
        pltpu.make_async_copy(stage.at[q], stage.at[q], y_recv.at[q]).wait()

    pltpu.make_async_copy(stage.at[T_OTHER], stage.at[T_OTHER], c_recv.at[0]).wait()

    def g_copy(k):
        return pltpu.make_async_remote_copy(
            src_ref=stage,
            dst_ref=allst.at[g],
            send_sem=g_send.at[k],
            recv_sem=g_recv.at[g],
            device_id=((g + k) % NB, r, y),
            device_id_type=MESH,
        )

    @pl.loop(1, NB)
    def _(k):
        g_copy(k).start()

    allst[g] = stage[...]

    @pl.loop(1, NB)
    def _(k):
        b = (g + k) % NB
        pltpu.make_async_copy(allst.at[b], allst.at[b], g_recv.at[b]).wait()

    inv_b = []
    lds_b = []
    for b in range(NB):
        tile = allst[b, T_LD]
        inv_b.append(jnp.sum(jnp.sum(recip(tile), axis=0, keepdims=True), axis=1, keepdims=True))
        lds_b.append(jnp.sum(jnp.sum(tile, axis=0, keepdims=True), axis=1, keepdims=True))
    inv_t = functools.reduce(jnp.add, inv_b)
    lds_t = functools.reduce(jnp.add, lds_b)

    def slope(inv, ld, sums, count):
        return (inv * sums[4:8] - count * sums[0:4]) / (inv * ld - count * count)

    n_full = float(SNP * NB)
    n_del = float(SNP * (NB - 1))

    def total_of(q):
        total = allst[0, q]
        for b in range(1, NB):
            total = total + allst[b, q]
        return total

    def scaled(h):
        return lax.rsqrt(jnp.maximum(h, floor_value))

    for q in range(NQ):
        h = jnp.maximum(slope(inv_t, lds_t, total_of(q), n_full), 0.0)
        for c in range(NX):
            hrow[q * NX + c] = h[c : c + 1, :]

    for cb, q in ((r, y), (other, T_OTHER)):
        h_full = slope(inv_t, lds_t, total_of(q), n_full)
        hcols[cb, TROWS - 8 : TROWS, :] = jnp.zeros((8, TB), f32)
        for c in range(NX):
            lanes = slice(c * LANE, (c + 1) * LANE)
            hcols[cb, R_FULL : R_FULL + 1, lanes] = scaled(h_full[c : c + 1, :])
            hcols[cb, R_POS : R_POS + 1, lanes] = jnp.maximum(h_full[c : c + 1, :], 0.0)

    def weigh_columns(src, cb):
        @pl.loop(0, NCH)
        def _(s):
            rows = pl.ds(pl.multiple_of(s * LANE, LANE), LANE)
            for c in range(TB // LANE):
                lanes = slice(c * LANE, (c + 1) * LANE)
                h = hcols[cb, R_POS : R_POS + 1, lanes]
                u = recip(1.0 + h * ldcol[rows, :]).astype(bf16).astype(f32)
                colw[cb, rows, lanes] = (src[rows, lanes].astype(f32) * u).astype(bf16)

    weigh_columns(z_ref, r)
    pltpu.make_async_copy(cbuf, cbuf, c_recv.at[1]).wait()
    weigh_columns(cbuf, other)

    pass_on(0)
    send_chunk(2)

    def pair_copy(q, c):
        return pltpu.make_async_remote_copy(
            src_ref=sendy.at[q * NX + c],
            dst_ref=recvy.at[g],
            send_sem=a_send.at[q * NX + c],
            recv_sem=a_recv.at[g],
            device_id=(q * NX + c, r, y),
            device_id_type=MESH,
        )

    def extra_copy(c):
        return pltpu.make_async_remote_copy(
            src_ref=sendx.at[c],
            dst_ref=recvx.at[g],
            send_sem=e_send.at[c],
            recv_sem=e_recv.at[g],
            device_id=(y * NX + c, r, y),
            device_id_type=MESH,
        )

    def contract(left, right):
        return lax.dot_general(left, right, (((0,), (0,)), ((), ())), preferred_element_type=f32)

    def chunk_lanes(c):
        return pl.ds(pl.multiple_of((c % NX) * LANE, LANE), LANE)

    def half_lanes(side):
        return pl.ds(pl.multiple_of(side * HALF, HALF), HALF)

    def weigh_rows(q, c):
        h = hrow[q * NX + c]
        for s in range(NCH):
            rows = slice(s * LANE, (s + 1) * LANE)
            u = recip(1.0 + h * ldcol[rows, :]).astype(bf16).astype(f32)
            value = rbuf[q, c, rows, :].astype(f32) * u
            lhsy[rows, 0:LANE] = (value * lwcol[rows, :]).astype(bf16)
            lhsy[rows, LANE : 2 * LANE] = value.astype(bf16)

    def deliver(sums, q, c, send, recv, slot, copy):
        mine = q * NX + c == g

        @pl.when(mine)
        def _():
            recv[g, 0] = sums[0:ROWS]
            recv[g, 1] = sums[ROWS : 2 * ROWS]

        @pl.when(jnp.logical_not(mine))
        def _():
            send[slot, 0] = sums[0:ROWS]
            send[slot, 1] = sums[ROWS : 2 * ROWS]
            copy.start()

    def pair_sums(q, c):
        weigh_rows(q, c)
        cb = jnp.where(q > y, other, r)
        sums = contract(lhsy[...], colw[cb]).astype(bf16)
        deliver(sums, q, c, sendy, recvy, q * NX + c, pair_copy(q, c))

    def own_sums(c):
        weigh_rows(y, c)
        cols = jnp.concatenate(
            [
                colw[other, :, half_lanes((c // 2 + r) % 2)],
                colw[r, :, chunk_lanes(c)],
                colw[r, :, chunk_lanes(c + 1)],
            ],
            axis=1,
        )
        sums = contract(lhsy[...], cols).astype(bf16)
        deliver(sums, y, c, sendy, recvy, y * NX + c, pair_copy(y, c))

        @pl.when(c < 2)
        def _():
            extra = contract(lhsy[...], colw[r, :, chunk_lanes(c + 2)]).astype(bf16)
            deliver(extra, y, c, sendx, recvx, c, extra_copy(c))

    @pl.loop(0, NX)
    def _(step):
        own_sums(chunk_of(step))

    def make_table(rows):
        @pl.when(jnp.logical_not(diag))
        def _():
            ctab[rows, 0:TB] = hcols[own_cb, rows, :]
            ctab[rows, TB : TB + LANE] = hcols[own_cb, rows, 0:LANE]

        @pl.when(diag)
        def _():
            ctab[rows, 0:HALF] = hcols[other, rows, half_lanes(half)]
            for i in range(3):
                ctab[rows, HALF + i * LANE : HALF + (i + 1) * LANE] = hcols[
                    r, rows, chunk_lanes(x + i)
                ]

    make_table(slice(TROWS - 8, TROWS))
    hdr[...] = jnp.zeros((LANE, LANE), f32)
    hdr[R_POS : R_POS + 1, :] = hrow[zz * NX + x]
    hdt[...] = jnp.transpose(hdr[...])

    def weight_sums(b):
        tile = allst[b, T_LD]
        inv = recip(tile)
        h = hdt[:, R_POS : R_POS + 1]
        for c in range(NCH):
            lanes = slice(c * LANE, (c + 1) * LANE)
            row = tile[c : c + 1, :]
            u16 = recip(1.0 + h * row).astype(bf16)
            u = u16.astype(f32)
            lhsw[0:ROWS, lanes] = (u * inv[c : c + 1, :]).astype(bf16)
            lhsw[ROWS : 2 * ROWS, lanes] = u16
            lhsw[2 * ROWS : 3 * ROWS, lanes] = (u * row).astype(bf16)
        ldc = column_tile(tile)
        h = ctab[R_POS : R_POS + 1, 0:TB]
        for c in range(NCH):
            ucol[c * LANE : (c + 1) * LANE, :] = recip(1.0 + ldc[:, c : c + 1] * h).astype(bf16)
        wbuf[b] = jnp.dot(lhsw[...], ucol[...], preferred_element_type=f32)

        @pl.when(fifth)
        def _():
            h = ctab[R_POS : R_POS + 1, TB : TB + LANE]
            for c in range(NCH):
                ucol[c * LANE : (c + 1) * LANE, 0:LANE] = recip(1.0 + ldc[:, c : c + 1] * h).astype(
                    bf16
                )
            wext[b] = jnp.dot(lhsw[...], ucol[:, 0:LANE], preferred_element_type=f32)

    @pl.loop(0, NX)
    def _(step):
        @pl.when(step < NX - 1)
        def _():
            pass_on(step + 1)

        @pl.when(step == 0)
        def _():
            send_chunk(NX - 1)

        c = chunk_of(step)
        far = (y + 2) % NQ
        for way in range(2):
            part = rbuf.at[far, c, pl.ds(way * (SNP // 2), SNP // 2)]
            pltpu.make_async_copy(part, part, f_recv.at[way, c]).wait()

        @pl.loop(1, NQ)
        def _(k):
            pair_sums((y + k) % NQ, c)

        @pl.loop(0, NB // NX)
        def _(k):
            weight_sums(step * (NB // NX) + k)

    for cb, q in ((r, y), (other, T_OTHER)):
        total = total_of(q)
        for b in range(NB):
            h = scaled(slope(inv_t - inv_b[b], lds_t - lds_b[b], total - allst[b, q], n_del))
            for c in range(NX):
                hcols[cb, b : b + 1, c * LANE : (c + 1) * LANE] = h[c : c + 1, :]
    make_table(slice(0, NB))
    total = total_of(zz)
    h_full = scaled(slope(inv_t, lds_t, total, n_full))
    for c in range(NX):
        hdq[R_FULL, c] = h_full[c : c + 1, :]
    for b in range(NB):
        h = scaled(slope(inv_t - inv_b[b], lds_t - lds_b[b], total - allst[b, zz], n_del))
        for c in range(NX):
            hdq[b, c] = h[c : c + 1, :]
    for b in range(NB + 1):
        hdr[b : b + 1, :] = hdq[b, x]
    hdt[...] = jnp.transpose(hdr[...])

    def factors(weights, full, first, width):
        @pl.loop(0, ROWS // 8)
        def _(t):
            base = pl.multiple_of(t * 8, 8)

            def at(i):
                return pl.ds(i * ROWS + base, 8)

            for c in range(width // LANE):
                lanes = slice(c * LANE, (c + 1) * LANE)
                tlanes = slice(first + c * LANE, first + (c + 1) * LANE)
                tot = [weights[0, at(i), lanes] for i in range(3)]
                for b in range(1, NB):
                    tot = [tot[i] + weights[b, at(i), lanes] for i in range(3)]

                def pair(w, b):
                    scale = hdt[pl.ds(base, 8), b : b + 1] * ctab[b : b + 1, tlanes]
                    k = scale / (w[0] * w[2] - w[1] * w[1])
                    return w[0] * k, w[1] * k

                full[0, pl.ds(base, 8), lanes], full[1, pl.ds(base, 8), lanes] = pair(tot, R_FULL)
                for b in range(NB):
                    w = [tot[i] - weights[b, at(i), lanes] for i in range(3)]
                    weights[b, at(0), lanes], weights[b, at(1), lanes] = pair(w, b)

    factors(wbuf, wfull, 0, TB)

    @pl.when(fifth)
    def _():
        factors(wext, wfext, TB, LANE)

    def place(j):
        on_half = j < 2
        cb = jnp.where(jnp.logical_not(diag), own_cb, jnp.where(on_half, other, r))
        chunk = jnp.where(
            jnp.logical_not(diag), j, jnp.where(on_half, 2 * half + j, (x + j + 2) % NX)
        )
        return cb, chunk

    def mirror_copy(j):
        cb, chunk = place(j)
        slot = jnp.where(jnp.logical_and(diag, j >= 2), j + 1, x)
        return pltpu.make_async_remote_copy(
            src_ref=msend.at[j],
            dst_ref=mrecv.at[slot],
            send_sem=m_send.at[j],
            recv_sem=m_recv.at[slot],
            device_id=(y * NX + chunk, cb, zz),
            device_id_type=MESH,
        )

    def sends(j):
        return jnp.logical_not(jnp.logical_and(diag, j == 2))

    def finish(pairs, weights, full, j, first):
        cb, chunk = place(j)
        out = chunk_lanes(chunk)
        lanes = pl.ds(pl.multiple_of(first, LANE), LANE)

        @pl.loop(0, ROWS // 16)
        def _(t):
            base = pl.multiple_of(t * 16, 16)
            rows = pl.ds(base, 16)
            tot0 = pairs[0, 0, rows, lanes].astype(f32)
            tot1 = pairs[0, 1, rows, lanes].astype(f32)
            for b in range(1, NB):
                tot0 = tot0 + pairs[b, 0, rows, lanes].astype(f32)
                tot1 = tot1 + pairs[b, 1, rows, lanes].astype(f32)
            rg_ref[cb, rows, out] = full[0, rows, lanes] * tot1 - full[1, rows, lanes] * tot0
            values = []
            for b in range(NB):
                del0 = tot0 - pairs[b, 0, rows, lanes].astype(f32)
                del1 = tot1 - pairs[b, 1, rows, lanes].astype(f32)
                values.append(
                    weights[b, pl.ds(base, 16), lanes] * del1
                    - weights[b, pl.ds(ROWS + base, 16), lanes] * del0
                )
            mean = functools.reduce(jnp.add, values) * (1.0 / NB)
            spread = functools.reduce(jnp.add, [(v - mean) * (v - mean) for v in values])
            se_ref[cb, rows, out] = jnp.sqrt((NB - 1) / NB * spread)

        @pl.when(sends(j))
        def _():
            msend[j, 0] = jnp.transpose(rg_ref[cb, :, out]).astype(bf16)
            msend[j, 1] = jnp.transpose(se_ref[cb, :, out]).astype(bf16)
            mirror_copy(j).start()

    @pl.loop(1, NB)
    def _(k):
        b = (g + k) % NB
        pltpu.make_async_copy(recvy.at[b], recvy.at[b], a_recv.at[b]).wait()

    @pl.loop(0, NX)
    def _(j):
        finish(recvy, wbuf, wfull, j, j * LANE)

    @pl.when(fifth)
    def _():
        @pl.loop(1, NB)
        def _(k):
            b = (g + k) % NB
            pltpu.make_async_copy(recvx.at[b], recvx.at[b], e_recv.at[b]).wait()

        finish(recvx, wext, wfext, NX, 0)

    def take(slot, cb, chunk):
        pltpu.make_async_copy(mrecv.at[slot], mrecv.at[slot], m_recv.at[slot]).wait()
        rg_ref[cb, :, chunk_lanes(chunk)] = mrecv[slot, 0].astype(f32)
        se_ref[cb, :, chunk_lanes(chunk)] = mrecv[slot, 1].astype(f32)

    @pl.when(jnp.logical_not(diag))
    def _():
        @pl.loop(0, NX)
        def _(k):
            take(k, 1 - own_cb, k)

    @pl.when(diag)
    def _():
        @pl.loop(0, 2)
        def _(k):
            chunk = 2 * (1 - half) + k
            take(chunk, other, chunk)

        take(NX, r, x + 3)

        @pl.when(x >= 2)
        def _():
            take(NX + 1, r, x + 2)

    @pl.loop(1, NQ)
    def _(k):
        y_copy(k).wait_send()

    core_copy(stage.at[y], stage.at[T_OTHER], 0).wait_send()
    core_copy(z_ref, cbuf, 1).wait_send()

    @pl.loop(0, NX)
    def _(c):
        for way in range(2):
            row_copy(way, c).wait_send()
            far_copy(way, c).wait_send()

    @pl.loop(1, NB)
    def _(k):
        g_copy(k).wait_send()
        p = (g + k) % NB
        pair_copy(p // NX, p % NX).wait_send()

    @pl.loop(0, 2)
    def _(c):
        @pl.when(y * NX + c != g)
        def _():
            extra_copy(c).wait_send()

    @pl.loop(0, NX)
    def _(j):
        @pl.when(sends(j))
        def _():
            mirror_copy(j).wait_send()

    @pl.when(fifth)
    def _():
        mirror_copy(NX).wait_send()


def per_device(ldscore, zscores):
    dma = pltpu.SemaphoreType.DMA
    out = jax.ShapeDtypeStruct((2, ROWS, TB), f32)
    rg, se = pl.pallas_call(
        kernel,
        out_shape=(out, out),
        in_specs=[pl.BlockSpec(memory_space=pltpu.VMEM)] * 2,
        out_specs=[pl.BlockSpec(memory_space=pltpu.VMEM)] * 2,
        scratch_shapes=[
            pltpu.VMEM((T_LD + 1, 8, LANE), f32),
            pltpu.VMEM((NB, T_LD + 1, 8, LANE), f32),
            pltpu.VMEM((SNP, LANE), f32),
            pltpu.VMEM((SNP, LANE), f32),
            pltpu.VMEM((NQ * NX, 1, LANE), f32),
            pltpu.VMEM((R_POS + 1, NX, 1, LANE), f32),
            pltpu.VMEM((LANE, LANE), f32),
            pltpu.VMEM((LANE, LANE), f32),
            pltpu.VMEM((2, TROWS, TB), f32),
            pltpu.VMEM((TROWS, TB + LANE), f32),
            pltpu.VMEM((NQ, NX, SNP, LANE), bf16),
            pltpu.VMEM((SNP, TB), bf16),
            pltpu.VMEM((2, SNP, TB), bf16),
            pltpu.VMEM((SNP, 2 * LANE), bf16),
            pltpu.VMEM((NB, 2, ROWS, TB), bf16),
            pltpu.VMEM((2, 2, ROWS, LANE), bf16),
            pltpu.VMEM((NB, 2, ROWS, TB), bf16),
            pltpu.VMEM((NB, 2, ROWS, LANE), bf16),
            pltpu.VMEM((3 * ROWS, SNP), bf16),
            pltpu.VMEM((SNP, TB), bf16),
            pltpu.VMEM((NB, 3 * ROWS, TB), f32),
            pltpu.VMEM((NB, 3 * ROWS, LANE), f32),
            pltpu.VMEM((2, ROWS, TB), f32),
            pltpu.VMEM((2, ROWS, LANE), f32),
            pltpu.VMEM((NX + 1, 2, LANE, LANE), bf16),
            pltpu.VMEM((NX + 2, 2, LANE, LANE), bf16),
            dma((NQ,)),
            dma((NQ,)),
            dma((NB,)),
            dma((NB,)),
            dma((2,)),
            dma((2,)),
            dma((2, NX)),
            dma((2, NX)),
            dma((2, NX)),
            dma((2, NX)),
            dma((NB,)),
            dma((NB,)),
            dma((2,)),
            dma((NB,)),
            dma((NX + 1,)),
            dma((NX + 2,)),
        ],
        compiler_params=pltpu.CompilerParams(
            collective_id=0, has_side_effects=True, vmem_limit_bytes=56 * 1024 * 1024
        ),
    )(ldscore.reshape(8, LANE), zscores)
    return (rg.transpose(1, 0, 2)[None], se.transpose(1, 0, 2)[None])


def solution(mesh):
    return jax.shard_map(
        per_device,
        mesh=mesh,
        in_specs=(P("genome"), P("genome", ("trow", "tcol"))),
        out_specs=(P("trow", "genome", None, "tcol"), P("trow", "genome", None, "tcol")),
        check_vma=False,
    )
```

time: 127 us -> 119 us (0.937)
  the two profiles are of different devices: /device:TPU:102 before, /device:TPU:38 now
where the time goes in v2:
time: 119 us; the launch traced here: 118 us
  Pallas kernels  114 us (96%)
  local copies, waits for them, and re-layouts  3.5 us (3%)
    pallas_call x1, Pallas kernels, per_device(): pl.pallas_call(kernel, out_shape=(out, out), in_specs=[pl.BlockSpec(memor...  114 us
    unnamed x4, local copies, waits for them, and re-layouts  3.5 us

profile of v2, /device:TPU:38, one launch (start us, length us, event | category | flops | bytes accessed | tf_op | source)
XLA Modules:
  0.0 118.4 jit_solution(5135005273623250168)
XLA Ops:
  0.6 114.3 %shard_map.41 = (f32[2,128,512]{2,1,0:T(8,128)}, f32[2,128,512]{2,1,0:T(8,128)}) custom-call(f32[8,128]{1,0:T(8,128)} %bitcast.9, bf16[1024,512]{1,0:T(8,128)(2,1)} %z_ref.1), custom_call_target="tpu_custom_call" | custom-call | tf_op jit(solution)/shard_map/pallas_call | solution.py:644
  114.9 0.0 copy-start
  114.9 2.3 %copy.4 = f32[1,128,2,512]{3,2,1,0:T(2,128)} copy(f32[1,128,2,512]{3,1,2,0:T(8,128)} %bitcast.8) | data formatting | bytes 1048576
  117.2 0.0 copy-done
  117.2 1.2 %copy.5 = f32[1,128,2,512]{3,2,1,0:T(2,128)} copy(f32[1,128,2,512]{3,1,2,0:T(8,128)S(1)} %bitcast.7) | data formatting | bytes 1048576
Async XLA Ops:
  114.9 2.3 %copy-start = (f32[2,128,512]{2,1,0:T(8,128)S(1)}, f32[2,128,512]{2,1,0:T(8,128)}, u32[]{:S(2)}) copy-start(f32[2,128,512]{2,1,0:T(8,128)} %get-tuple-element.5) | copy-start | bytes 1572868

commit v3 on v2

--- a/solution.py
+++ b/solution.py
@@ -28,6 +28,15 @@
 
 T_OTHER = NQ
 T_LD = NQ + 1
+
+W_STEP = 3
+
+NT = 4
+PART = ROWS // NT
+ORDER = (
+    (2, 2), (1, 1), (3, 3), (1, 3), (3, 1), (1, 2), (3, 2), (2, 1), (2, 3),
+    (0, 1), (1, 0), (0, 3), (3, 0), (0, 2), (2, 0),
+)
 
 
 def recip(value):
@@ -48,6 +57,7 @@
     ldcol,
     lwcol,
     hrow,
+    hpos,
     hdq,
     hdr,
     hdt,
@@ -137,15 +147,25 @@
         acc_l = jnp.zeros((8, LANE), f32)
         for s in range(NCH):
             rows = slice(s * LANE, (s + 1) * LANE)
-            zraw = z_ref[rows, lanes]
-            rbuf[y, c, rows, :] = zraw
-            zc = zraw.astype(f32)
+            zc = z_ref[rows, lanes].astype(f32)
             sq = zc * zc
             acc_l = acc_l + jnp.sum(sq.reshape(LANE // 8, 8, LANE), axis=0)
             acc_y = acc_y + jnp.sum((sq * lwcol[rows, :]).reshape(LANE // 8, 8, LANE), axis=0)
         stage[y, c : c + 1, :] = jnp.sum(acc_y, axis=0, keepdims=True)
         stage[y, 4 + c : 5 + c, :] = jnp.sum(acc_l, axis=0, keepdims=True)
     stage[T_LD] = ld_tile
+
+    def gather_parts(value, t):
+        return jnp.concatenate(
+            [value[:, c * LANE + t * PART : c * LANE + (t + 1) * PART] for c in range(NX)], axis=1
+        )
+
+    def make_chunk(t):
+        for s in range(NCH):
+            rows = slice(s * LANE, (s + 1) * LANE)
+            rbuf[y, t, rows, :] = gather_parts(z_ref[rows, :], t)
+
+    make_chunk(0)
 
     @pl.when(diag)
     def _():
@@ -181,9 +201,6 @@
 
     core_copy(stage.at[y], stage.at[T_OTHER], 0).start()
     core_copy(z_ref, cbuf, 1).start()
-
-    def chunk_of(step):
-        return (x + 3 * step + 2) % NX
 
     def row_copy(way, c):
         return pltpu.make_async_remote_copy(
@@ -208,19 +225,19 @@
         )
 
     def send_chunk(step):
-        c = chunk_of(step)
-        row_copy(0, c).start()
-        row_copy(1, c).start()
+        row_copy(0, step).start()
+        row_copy(1, step).start()
 
     def pass_on(step):
-        c = chunk_of(step)
         for way in range(2):
             q = (y + 3 + 2 * way) % NQ
-            pltpu.make_async_copy(rbuf.at[q, c], rbuf.at[q, c], r_recv.at[way, c]).wait()
-            far_copy(way, c).start()
+            pltpu.make_async_copy(
+                rbuf.at[q, step], rbuf.at[q, step], r_recv.at[way, step]
+            ).wait()
+            far_copy(way, step).start()
 
     send_chunk(0)
-    send_chunk(1)
+    make_chunk(1)
 
     @pl.loop(1, NQ)
     def _(k):
@@ -243,7 +260,11 @@
     def _(k):
         g_copy(k).start()
 
+    send_chunk(1)
     allst[g] = stage[...]
+    make_chunk(2)
+    make_chunk(3)
+    pass_on(0)
 
     @pl.loop(1, NB)
     def _(k):
@@ -277,7 +298,11 @@
     for q in range(NQ):
         h = jnp.maximum(slope(inv_t, lds_t, total_of(q), n_full), 0.0)
         for c in range(NX):
-            hrow[q * NX + c] = h[c : c + 1, :]
+            hpos[q * NX + c] = h[c : c + 1, :]
+        for t in range(NT):
+            hrow[q * NT + t] = jnp.concatenate(
+                [h[c : c + 1, t * PART : (t + 1) * PART] for c in range(NX)], axis=1
+            )
 
     for cb, q in ((r, y), (other, T_OTHER)):
         h_full = slope(inv_t, lds_t, total_of(q), n_full)
@@ -301,25 +326,27 @@
     pltpu.make_async_copy(cbuf, cbuf, c_recv.at[1]).wait()
     weigh_columns(cbuf, other)
 
-    pass_on(0)
     send_chunk(2)
 
-    def pair_copy(q, c):
+    def part_rows(t):
+        return pl.ds(pl.multiple_of(t * PART, PART), PART)
+
+    def pair_copy(q, c, t):
         return pltpu.make_async_remote_copy(
-            src_ref=sendy.at[q * NX + c],
-            dst_ref=recvy.at[g],
-            send_sem=a_send.at[q * NX + c],
-            recv_sem=a_recv.at[g],
+            src_ref=sendy.at[q * NX + c, :, part_rows(t)],
+            dst_ref=recvy.at[g, :, part_rows(t)],
+            send_sem=a_send.at[q * NX + c, t],
+            recv_sem=a_recv.at[g, t],
             device_id=(q * NX + c, r, y),
             device_id_type=MESH,
         )
 
-    def extra_copy(c):
+    def extra_copy(c, t):
         return pltpu.make_async_remote_copy(
-            src_ref=sendx.at[c],
-            dst_ref=recvx.at[g],
-            send_sem=e_send.at[c],
-            recv_sem=e_recv.at[g],
+            src_ref=sendx.at[c, :, part_rows(t)],
+            dst_ref=recvx.at[g, :, part_rows(t)],
+            send_sem=e_send.at[c, t],
+            recv_sem=e_recv.at[g, t],
             device_id=(y * NX + c, r, y),
             device_id_type=MESH,
         )
@@ -333,56 +360,61 @@
     def half_lanes(side):
         return pl.ds(pl.multiple_of(side * HALF, HALF), HALF)
 
-    def weigh_rows(q, c):
-        h = hrow[q * NX + c]
+    def weigh_rows(q, t):
+        h = hrow[q * NT + t]
         for s in range(NCH):
             rows = slice(s * LANE, (s + 1) * LANE)
             u = recip(1.0 + h * ldcol[rows, :]).astype(bf16).astype(f32)
-            value = rbuf[q, c, rows, :].astype(f32) * u
+            value = rbuf[q, t, rows, :].astype(f32) * u
             lhsy[rows, 0:LANE] = (value * lwcol[rows, :]).astype(bf16)
             lhsy[rows, LANE : 2 * LANE] = value.astype(bf16)
 
-    def deliver(sums, q, c, send, recv, slot, copy):
-        mine = q * NX + c == g
-
-        @pl.when(mine)
-        def _():
-            recv[g, 0] = sums[0:ROWS]
-            recv[g, 1] = sums[ROWS : 2 * ROWS]
-
-        @pl.when(jnp.logical_not(mine))
-        def _():
-            send[slot, 0] = sums[0:ROWS]
-            send[slot, 1] = sums[ROWS : 2 * ROWS]
-            copy.start()
-
-    def pair_sums(q, c):
-        weigh_rows(q, c)
+    def pair_sums(q, t):
+        weigh_rows(q, t)
         cb = jnp.where(q > y, other, r)
         sums = contract(lhsy[...], colw[cb]).astype(bf16)
-        deliver(sums, q, c, sendy, recvy, q * NX + c, pair_copy(q, c))
-
-    def own_sums(c):
-        weigh_rows(y, c)
-        cols = jnp.concatenate(
-            [
-                colw[other, :, half_lanes((c // 2 + r) % 2)],
-                colw[r, :, chunk_lanes(c)],
-                colw[r, :, chunk_lanes(c + 1)],
-            ],
-            axis=1,
-        )
-        sums = contract(lhsy[...], cols).astype(bf16)
-        deliver(sums, y, c, sendy, recvy, y * NX + c, pair_copy(y, c))
-
-        @pl.when(c < 2)
-        def _():
-            extra = contract(lhsy[...], colw[r, :, chunk_lanes(c + 2)]).astype(bf16)
-            deliver(extra, y, c, sendx, recvx, c, extra_copy(c))
-
-    @pl.loop(0, NX)
-    def _(step):
-        own_sums(chunk_of(step))
+        for c in range(NX):
+            for i in range(2):
+                first = i * LANE + c * PART
+                sendy[q * NX + c, i, part_rows(t), :] = sums[first : first + PART]
+
+    def own_sums(t):
+        weigh_rows(y, t)
+        own = contract(lhsy[...], colw[r]).astype(bf16)
+        cross = contract(lhsy[...], colw[other])
+        low, high = cross[:, 0:HALF], cross[:, HALF:TB]
+        sides = (
+            jnp.where(r == 0, low, high).astype(bf16),
+            jnp.where(r == 0, high, low).astype(bf16),
+        )
+        for c in range(NX):
+            near, after = (c + 1) % NX * LANE, (c + 2) % NX * LANE
+            for i in range(2):
+                rows = slice(i * LANE + c * PART, i * LANE + (c + 1) * PART)
+                dst = y * NX + c
+                sendy[dst, i, part_rows(t), 0:HALF] = sides[c // 2][rows]
+                sendy[dst, i, part_rows(t), HALF : HALF + LANE] = own[
+                    rows, c * LANE : (c + 1) * LANE
+                ]
+                sendy[dst, i, part_rows(t), HALF + LANE : TB] = own[rows, near : near + LANE]
+                if c < 2:
+                    sendx[c, i, part_rows(t), :] = own[rows, after : after + LANE]
+
+    def deliver(t):
+        for dz, dx in ORDER:
+            pair_copy((zz + dz) % NQ, (x + dx) % NX, t).start()
+
+        recvy[g, :, part_rows(t), :] = sendy[g, :, part_rows(t), :]
+
+        @pl.loop(0, 2)
+        def _(c):
+            @pl.when(y * NX + c == g)
+            def _():
+                recvx[g, :, part_rows(t), :] = sendx[c, :, part_rows(t), :]
+
+            @pl.when(y * NX + c != g)
+            def _():
+                extra_copy(c, t).start()
 
     def make_table(rows):
         @pl.when(jnp.logical_not(diag))
@@ -400,7 +432,7 @@
 
     make_table(slice(TROWS - 8, TROWS))
     hdr[...] = jnp.zeros((LANE, LANE), f32)
-    hdr[R_POS : R_POS + 1, :] = hrow[zz * NX + x]
+    hdr[R_POS : R_POS + 1, :] = hpos[zz * NX + x]
     hdt[...] = jnp.transpose(hdr[...])
 
     def weight_sums(b):
@@ -432,27 +464,38 @@
 
     @pl.loop(0, NX)
     def _(step):
-        @pl.when(step < NX - 1)
-        def _():
-            pass_on(step + 1)
-
-        @pl.when(step == 0)
-        def _():
-            send_chunk(NX - 1)
-
-        c = chunk_of(step)
         far = (y + 2) % NQ
         for way in range(2):
-            part = rbuf.at[far, c, pl.ds(way * (SNP // 2), SNP // 2)]
-            pltpu.make_async_copy(part, part, f_recv.at[way, c]).wait()
-
-        @pl.loop(1, NQ)
+            part = rbuf.at[far, step, pl.ds(way * (SNP // 2), SNP // 2)]
+            pltpu.make_async_copy(part, part, f_recv.at[way, step]).wait()
+
+        @pl.loop(0, NQ)
         def _(k):
-            pair_sums((y + k) % NQ, c)
-
-        @pl.loop(0, NB // NX)
+            @pl.when(k == y)
+            def _():
+                own_sums(step)
+
+            @pl.when(k != y)
+            def _():
+                pair_sums(k, step)
+
+        deliver(step)
+
+        @pl.when(step < NT - 1)
+        def _():
+            pass_on(step + 1)
+
+        @pl.loop(0, W_STEP)
         def _(k):
-            weight_sums(step * (NB // NX) + k)
+            weight_sums(step * W_STEP + k)
+
+        @pl.when(step == 0)
+        def _():
+            send_chunk(NT - 1)
+
+    @pl.loop(NT * W_STEP, NB)
+    def _(b):
+        weight_sums(b)
 
     for cb, q in ((r, y), (other, T_OTHER)):
         total = total_of(q)
@@ -512,14 +555,14 @@
         )
         return cb, chunk
 
-    def mirror_copy(j):
+    def mirror_copy(j, t):
         cb, chunk = place(j)
         slot = jnp.where(jnp.logical_and(diag, j >= 2), j + 1, x)
         return pltpu.make_async_remote_copy(
-            src_ref=msend.at[j],
-            dst_ref=mrecv.at[slot],
-            send_sem=m_send.at[j],
-            recv_sem=m_recv.at[slot],
+            src_ref=msend.at[j, :, part_rows(t)],
+            dst_ref=mrecv.at[slot, :, part_rows(t)],
+            send_sem=m_send.at[j, t],
+            recv_sem=m_recv.at[slot, t],
             device_id=(y * NX + chunk, cb, zz),
             device_id_type=MESH,
         )
@@ -527,21 +570,23 @@
     def sends(j):
         return jnp.logical_not(jnp.logical_and(diag, j == 2))
 
-    def finish(pairs, weights, full, j, first):
+    def finish(pairs, weights, full, j, first, t):
         cb, chunk = place(j)
         out = chunk_lanes(chunk)
         lanes = pl.ds(pl.multiple_of(first, LANE), LANE)
 
-        @pl.loop(0, ROWS // 16)
-        def _(t):
-            base = pl.multiple_of(t * 16, 16)
+        @pl.loop(0, PART // 16)
+        def _(i):
+            base = pl.multiple_of(t * PART + i * 16, 16)
             rows = pl.ds(base, 16)
             tot0 = pairs[0, 0, rows, lanes].astype(f32)
             tot1 = pairs[0, 1, rows, lanes].astype(f32)
             for b in range(1, NB):
                 tot0 = tot0 + pairs[b, 0, rows, lanes].astype(f32)
                 tot1 = tot1 + pairs[b, 1, rows, lanes].astype(f32)
-            rg_ref[cb, rows, out] = full[0, rows, lanes] * tot1 - full[1, rows, lanes] * tot0
+            rg = full[0, rows, lanes] * tot1 - full[1, rows, lanes] * tot0
+            rg_ref[cb, rows, out] = rg
+            msend[j, 0, rows, :] = rg.astype(bf16)
             values = []
             for b in range(NB):
                 del0 = tot0 - pairs[b, 0, rows, lanes].astype(f32)
@@ -552,36 +597,43 @@
                 )
             mean = functools.reduce(jnp.add, values) * (1.0 / NB)
             spread = functools.reduce(jnp.add, [(v - mean) * (v - mean) for v in values])
-            se_ref[cb, rows, out] = jnp.sqrt((NB - 1) / NB * spread)
+            se = jnp.sqrt((NB - 1) / NB * spread)
+            se_ref[cb, rows, out] = se
+            msend[j, 1, rows, :] = se.astype(bf16)
 
         @pl.when(sends(j))
         def _():
-            msend[j, 0] = jnp.transpose(rg_ref[cb, :, out]).astype(bf16)
-            msend[j, 1] = jnp.transpose(se_ref[cb, :, out]).astype(bf16)
-            mirror_copy(j).start()
-
-    @pl.loop(1, NB)
-    def _(k):
-        b = (g + k) % NB
-        pltpu.make_async_copy(recvy.at[b], recvy.at[b], a_recv.at[b]).wait()
-
-    @pl.loop(0, NX)
-    def _(j):
-        finish(recvy, wbuf, wfull, j, j * LANE)
-
-    @pl.when(fifth)
-    def _():
+            mirror_copy(j, t).start()
+
+    @pl.loop(0, NT)
+    def _(t):
         @pl.loop(1, NB)
         def _(k):
-            b = (g + k) % NB
-            pltpu.make_async_copy(recvx.at[b], recvx.at[b], e_recv.at[b]).wait()
-
-        finish(recvx, wext, wfext, NX, 0)
+            part = recvy.at[(g + k) % NB, :, part_rows(t)]
+            pltpu.make_async_copy(part, part, a_recv.at[(g + k) % NB, t]).wait()
+
+        @pl.loop(0, NX)
+        def _(j):
+            finish(recvy, wbuf, wfull, j, j * LANE, t)
+
+        @pl.when(fifth)
+        def _():
+            @pl.loop(1, NB)
+            def _(k):
+                part = recvx.at[(g + k) % NB, :, part_rows(t)]
+                pltpu.make_async_copy(part, part, e_recv.at[(g + k) % NB, t]).wait()
+
+            finish(recvx, wext, wfext, NX, 0, t)
 
     def take(slot, cb, chunk):
-        pltpu.make_async_copy(mrecv.at[slot], mrecv.at[slot], m_recv.at[slot]).wait()
-        rg_ref[cb, :, chunk_lanes(chunk)] = mrecv[slot, 0].astype(f32)
-        se_ref[cb, :, chunk_lanes(chunk)] = mrecv[slot, 1].astype(f32)
+        @pl.loop(0, NT)
+        def _(t):
+            part = mrecv.at[slot, :, part_rows(t)]
+            pltpu.make_async_copy(part, part, m_recv.at[slot, t]).wait()
+
+        lanes = chunk_lanes(chunk)
+        rg_ref[cb, :, lanes] = jnp.transpose(mrecv[slot, 0].astype(f32))
+        se_ref[cb, :, lanes] = jnp.transpose(mrecv[slot, 1].astype(f32))
 
     @pl.when(jnp.logical_not(diag))
     def _():
@@ -619,23 +671,28 @@
     def _(k):
         g_copy(k).wait_send()
         p = (g + k) % NB
-        pair_copy(p // NX, p % NX).wait_send()
-
-    @pl.loop(0, 2)
-    def _(c):
-        @pl.when(y * NX + c != g)
-        def _():
-            extra_copy(c).wait_send()
-
-    @pl.loop(0, NX)
-    def _(j):
-        @pl.when(sends(j))
-        def _():
-            mirror_copy(j).wait_send()
-
-    @pl.when(fifth)
-    def _():
-        mirror_copy(NX).wait_send()
+
+        @pl.loop(0, NT)
+        def _(t):
+            pair_copy(p // NX, p % NX, t).wait_send()
+
+    @pl.loop(0, NT)
+    def _(t):
+        @pl.loop(0, 2)
+        def _(c):
+            @pl.when(y * NX + c != g)
+            def _():
+                extra_copy(c, t).wait_send()
+
+        @pl.loop(0, NX)
+        def _(j):
+            @pl.when(sends(j))
+            def _():
+                mirror_copy(j, t).wait_send()
+
+        @pl.when(fifth)
+        def _():
+            mirror_copy(NX, t).wait_send()
 
 
 def per_device(ldscore, zscores):
@@ -651,13 +708,14 @@
             pltpu.VMEM((NB, T_LD + 1, 8, LANE), f32),
             pltpu.VMEM((SNP, LANE), f32),
             pltpu.VMEM((SNP, LANE), f32),
+            pltpu.VMEM((NQ * NT, 1, LANE), f32),
             pltpu.VMEM((NQ * NX, 1, LANE), f32),
             pltpu.VMEM((R_POS + 1, NX, 1, LANE), f32),
             pltpu.VMEM((LANE, LANE), f32),
             pltpu.VMEM((LANE, LANE), f32),
             pltpu.VMEM((2, TROWS, TB), f32),
             pltpu.VMEM((TROWS, TB + LANE), f32),
-            pltpu.VMEM((NQ, NX, SNP, LANE), bf16),
+            pltpu.VMEM((NQ, NT, SNP, LANE), bf16),
             pltpu.VMEM((SNP, TB), bf16),
             pltpu.VMEM((2, SNP, TB), bf16),
             pltpu.VMEM((SNP, 2 * LANE), bf16),
@@ -679,16 +737,16 @@
             dma((NB,)),
             dma((2,)),
             dma((2,)),
-            dma((2, NX)),
-            dma((2, NX)),
-            dma((2, NX)),
-            dma((2, NX)),
-            dma((NB,)),
-            dma((NB,)),
-            dma((2,)),
-            dma((NB,)),
-            dma((NX + 1,)),
-            dma((NX + 2,)),
+            dma((2, NT)),
+            dma((2, NT)),
+            dma((2, NT)),
+            dma((2, NT)),
+            dma((NB, NT)),
+            dma((NB, NT)),
+            dma((2, NT)),
+            dma((NB, NT)),
+            dma((NX + 1, NT)),
+            dma((NX + 2, NT)),
         ],
         compiler_params=pltpu.CompilerParams(
             collective_id=0, has_side_effects=True, vmem_limit_bytes=56 * 1024 * 1024

time: 119 us -> 99.9 us (0.84)
  the two profiles are of different devices: /device:TPU:38 before, /device:TPU:17 now
where the time goes in v3:
time: 99.9 us; the launch traced here: 98.7 us
  Pallas kernels  94.6 us (95%)
  local copies, waits for them, and re-layouts  3.5 us (4%)
    pallas_call x1, Pallas kernels, per_device(): pl.pallas_call(kernel, out_shape=(out, out), in_specs=[pl.BlockSpec(memor...  94.6 us
    unnamed x4, local copies, waits for them, and re-layouts  3.5 us

profile of v3, /device:TPU:17, one launch (start us, length us, event | category | flops | bytes accessed | tf_op | source)
XLA Modules:
  0.0 98.7 jit_solution(4206050664008791447)
XLA Ops:
  0.6 94.6 %shard_map.41 = (f32[2,128,512]{2,1,0:T(8,128)}, f32[2,128,512]{2,1,0:T(8,128)}) custom-call(f32[8,128]{1,0:T(8,128)} %bitcast.9, bf16[1024,512]{1,0:T(8,128)(2,1)} %z_ref.1), custom_call_target="tpu_custom_call" | custom-call | tf_op jit(solution)/shard_map/pallas_call | solution.py:701
  95.2 0.0 copy-start
  95.2 2.3 %copy.4 = f32[1,128,2,512]{3,2,1,0:T(2,128)} copy(f32[1,128,2,512]{3,1,2,0:T(8,128)} %bitcast.8) | data formatting | bytes 1048576
  97.5 0.0 copy-done
  97.5 1.2 %copy.5 = f32[1,128,2,512]{3,2,1,0:T(2,128)} copy(f32[1,128,2,512]{3,1,2,0:T(8,128)S(1)} %bitcast.7) | data formatting | bytes 1048576
Async XLA Ops:
  95.2 2.3 %copy-start = (f32[2,128,512]{2,1,0:T(8,128)S(1)}, f32[2,128,512]{2,1,0:T(8,128)}, u32[]{:S(2)}) copy-start(f32[2,128,512]{2,1,0:T(8,128)} %get-tuple-element.5) | copy-start | bytes 1572868

commit v4 on v3

--- a/solution.py
+++ b/solution.py
@@ -20,7 +20,6 @@
 NQ = 4
 NX = 4
 ROWS = 128
-HALF = 256
 
 R_FULL = NB
 R_POS = NB + 1
@@ -29,7 +28,7 @@
 T_OTHER = NQ
 T_LD = NQ + 1
 
-W_STEP = 3
+W_STEP = 4
 
 NT = 4
 PART = ROWS // NT
@@ -37,6 +36,15 @@
     (2, 2), (1, 1), (3, 3), (1, 3), (3, 1), (1, 2), (3, 2), (2, 1), (2, 3),
     (0, 1), (1, 0), (0, 3), (3, 0), (0, 2), (2, 0),
 )
+
+DIAG = (
+    ((3, 4, 5, 6), (1, 2, 5, 6, 7), (0, 1, 6, 7, 2), (0, 1, 7, 4)),
+    ((0, 1, 4, 5, 6), (0, 5, 6, 7), (0, 3, 6, 7), (1, 2, 7, 4, 3)),
+)
+
+
+def digits(chunks):
+    return sum(d << (4 * i) for i, d in enumerate(chunks))
 
 
 def recip(value):
@@ -75,6 +83,8 @@
     ucol,
     wbuf,
     wext,
+    fbuf,
+    fext,
     wfull,
     wfext,
     msend,
@@ -104,8 +114,12 @@
     other = 1 - r
     diag = zz == y
     own_cb = jnp.where(zz > y, other, r)
-    half = (x // 2 + r) % 2
-    fifth = jnp.logical_and(diag, x < 2)
+    code = jnp.int32(0)
+    for core in range(2):
+        for at_x in range(NX):
+            here = jnp.logical_and(r == core, x == at_x)
+            code = jnp.where(here, digits(DIAG[core][at_x]), code)
+    fifth = jnp.logical_and(diag, ((x + 1) // 2 + r) % 2 == 1)
 
     barrier = pltpu.get_barrier_semaphore()
 
@@ -341,13 +355,16 @@
             device_id_type=MESH,
         )
 
-    def extra_copy(c, t):
+    def fifth_x(e):
+        return jnp.where(r == 0, 1 + e, 3 * e)
+
+    def extra_copy(e, t):
         return pltpu.make_async_remote_copy(
-            src_ref=sendx.at[c, :, part_rows(t)],
+            src_ref=sendx.at[e, :, part_rows(t)],
             dst_ref=recvx.at[g, :, part_rows(t)],
-            send_sem=e_send.at[c, t],
+            send_sem=e_send.at[e, t],
             recv_sem=e_recv.at[g, t],
-            device_id=(y * NX + c, r, y),
+            device_id=(y * NX + fifth_x(e), r, y),
             device_id_type=MESH,
         )
 
@@ -356,9 +373,6 @@
 
     def chunk_lanes(c):
         return pl.ds(pl.multiple_of((c % NX) * LANE, LANE), LANE)
-
-    def half_lanes(side):
-        return pl.ds(pl.multiple_of(side * HALF, HALF), HALF)
 
     def weigh_rows(q, t):
         h = hrow[q * NT + t]
@@ -380,25 +394,27 @@
 
     def own_sums(t):
         weigh_rows(y, t)
-        own = contract(lhsy[...], colw[r]).astype(bf16)
-        cross = contract(lhsy[...], colw[other])
-        low, high = cross[:, 0:HALF], cross[:, HALF:TB]
-        sides = (
-            jnp.where(r == 0, low, high).astype(bf16),
-            jnp.where(r == 0, high, low).astype(bf16),
-        )
-        for c in range(NX):
-            near, after = (c + 1) % NX * LANE, (c + 2) % NX * LANE
-            for i in range(2):
-                rows = slice(i * LANE + c * PART, i * LANE + (c + 1) * PART)
-                dst = y * NX + c
-                sendy[dst, i, part_rows(t), 0:HALF] = sides[c // 2][rows]
-                sendy[dst, i, part_rows(t), HALF : HALF + LANE] = own[
-                    rows, c * LANE : (c + 1) * LANE
-                ]
-                sendy[dst, i, part_rows(t), HALF + LANE : TB] = own[rows, near : near + LANE]
-                if c < 2:
-                    sendx[c, i, part_rows(t), :] = own[rows, after : after + LANE]
+        sums = (
+            contract(lhsy[...], colw[other]).astype(bf16),
+            contract(lhsy[...], colw[r]).astype(bf16),
+        )
+
+        def piece(core, c, k, i):
+            d = DIAG[core][c][k]
+            rows = slice(i * LANE + c * PART, i * LANE + (c + 1) * PART)
+            return sums[d // NX][rows, d % NX * LANE : (d % NX + 1) * LANE]
+
+        def pick(zero, one):
+            return jnp.where(r == 0, zero.astype(f32), one.astype(f32)).astype(bf16)
+
+        for i in range(2):
+            for c in range(NX):
+                for k in range(4):
+                    sendy[y * NX + c, i, part_rows(t), k * LANE : (k + 1) * LANE] = pick(
+                        piece(0, c, k, i), piece(1, c, k, i)
+                    )
+            for e in range(2):
+                sendx[e, i, part_rows(t), :] = pick(piece(0, 1 + e, 4, i), piece(1, 3 * e, 4, i))
 
     def deliver(t):
         for dz, dx in ORDER:
@@ -407,28 +423,24 @@
         recvy[g, :, part_rows(t), :] = sendy[g, :, part_rows(t), :]
 
         @pl.loop(0, 2)
-        def _(c):
-            @pl.when(y * NX + c == g)
+        def _(e):
+            @pl.when(y * NX + fifth_x(e) == g)
             def _():
-                recvx[g, :, part_rows(t), :] = sendx[c, :, part_rows(t), :]
-
-            @pl.when(y * NX + c != g)
+                recvx[g, :, part_rows(t), :] = sendx[e, :, part_rows(t), :]
+
+            @pl.when(y * NX + fifth_x(e) != g)
             def _():
-                extra_copy(c, t).start()
+                extra_copy(e, t).start()
+
+    def place(j):
+        d = (code >> (4 * j)) & 7
+        cb = jnp.where(diag, jnp.where(d >= NX, r, other), own_cb)
+        return cb, jnp.where(diag, d % NX, j % NX)
 
     def make_table(rows):
-        @pl.when(jnp.logical_not(diag))
-        def _():
-            ctab[rows, 0:TB] = hcols[own_cb, rows, :]
-            ctab[rows, TB : TB + LANE] = hcols[own_cb, rows, 0:LANE]
-
-        @pl.when(diag)
-        def _():
-            ctab[rows, 0:HALF] = hcols[other, rows, half_lanes(half)]
-            for i in range(3):
-                ctab[rows, HALF + i * LANE : HALF + (i + 1) * LANE] = hcols[
-                    r, rows, chunk_lanes(x + i)
-                ]
+        for k in range(NX + 1):
+            cb, chunk = place(k)
+            ctab[rows, k * LANE : (k + 1) * LANE] = hcols[cb, rows, chunk_lanes(chunk)]
 
     make_table(slice(TROWS - 8, TROWS))
     hdr[...] = jnp.zeros((LANE, LANE), f32)
@@ -516,7 +528,7 @@
         hdr[b : b + 1, :] = hdq[b, x]
     hdt[...] = jnp.transpose(hdr[...])
 
-    def factors(weights, full, first, width):
+    def factors(weights, parts, full, first, width):
         @pl.loop(0, ROWS // 8)
         def _(t):
             base = pl.multiple_of(t * 8, 8)
@@ -539,25 +551,17 @@
                 full[0, pl.ds(base, 8), lanes], full[1, pl.ds(base, 8), lanes] = pair(tot, R_FULL)
                 for b in range(NB):
                     w = [tot[i] - weights[b, at(i), lanes] for i in range(3)]
-                    weights[b, at(0), lanes], weights[b, at(1), lanes] = pair(w, b)
-
-    factors(wbuf, wfull, 0, TB)
+                    parts[b, at(0), lanes], parts[b, at(1), lanes] = pair(w, b)
+
+    factors(wbuf, fbuf, wfull, 0, TB)
 
     @pl.when(fifth)
     def _():
-        factors(wext, wfext, TB, LANE)
-
-    def place(j):
-        on_half = j < 2
-        cb = jnp.where(jnp.logical_not(diag), own_cb, jnp.where(on_half, other, r))
-        chunk = jnp.where(
-            jnp.logical_not(diag), j, jnp.where(on_half, 2 * half + j, (x + j + 2) % NX)
-        )
-        return cb, chunk
+        factors(wext, fext, wfext, TB, LANE)
 
     def mirror_copy(j, t):
         cb, chunk = place(j)
-        slot = jnp.where(jnp.logical_and(diag, j >= 2), j + 1, x)
+        slot = jnp.where(jnp.logical_and(diag, cb == r), NX + x, x)
         return pltpu.make_async_remote_copy(
             src_ref=msend.at[j, :, part_rows(t)],
             dst_ref=mrecv.at[slot, :, part_rows(t)],
@@ -568,7 +572,8 @@
         )
 
     def sends(j):
-        return jnp.logical_not(jnp.logical_and(diag, j == 2))
+        cb, chunk = place(j)
+        return jnp.logical_not(diag & (cb == r) & (chunk == x))
 
     def finish(pairs, weights, full, j, first, t):
         cb, chunk = place(j)
@@ -614,7 +619,7 @@
 
         @pl.loop(0, NX)
         def _(j):
-            finish(recvy, wbuf, wfull, j, j * LANE, t)
+            finish(recvy, fbuf, wfull, j, j * LANE, t)
 
         @pl.when(fifth)
         def _():
@@ -623,7 +628,7 @@
                 part = recvx.at[(g + k) % NB, :, part_rows(t)]
                 pltpu.make_async_copy(part, part, e_recv.at[(g + k) % NB, t]).wait()
 
-            finish(recvx, wext, wfext, NX, 0, t)
+            finish(recvx, fext, wfext, NX, 0, t)
 
     def take(slot, cb, chunk):
         @pl.loop(0, NT)
@@ -643,16 +648,18 @@
 
     @pl.when(diag)
     def _():
-        @pl.loop(0, 2)
-        def _(k):
-            chunk = 2 * (1 - half) + k
-            take(chunk, other, chunk)
-
-        take(NX, r, x + 3)
-
-        @pl.when(x >= 2)
-        def _():
-            take(NX + 1, r, x + 2)
+        chunks = 4 + jnp.where(fifth, 1, 0)
+
+        @pl.loop(0, 2 * NX)
+        def _(d):
+            taken = jnp.int32(0)
+            for k in range(NX + 1):
+                hit = ((code >> (4 * k)) & 7) == d
+                taken = taken + jnp.where(jnp.logical_and(hit, k < chunks), 1, 0)
+
+            @pl.when(taken == 0)
+            def _():
+                take(d, jnp.where(d >= NX, r, other), d % NX)
 
     @pl.loop(1, NQ)
     def _(k):
@@ -679,10 +686,10 @@
     @pl.loop(0, NT)
     def _(t):
         @pl.loop(0, 2)
-        def _(c):
-            @pl.when(y * NX + c != g)
+        def _(e):
+            @pl.when(y * NX + fifth_x(e) != g)
             def _():
-                extra_copy(c, t).wait_send()
+                extra_copy(e, t).wait_send()
 
         @pl.loop(0, NX)
         def _(j):
@@ -727,10 +734,12 @@
             pltpu.VMEM((SNP, TB), bf16),
             pltpu.VMEM((NB, 3 * ROWS, TB), f32),
             pltpu.VMEM((NB, 3 * ROWS, LANE), f32),
+            pltpu.VMEM((NB, 2 * ROWS, TB), f32),
+            pltpu.VMEM((NB, 2 * ROWS, LANE), f32),
             pltpu.VMEM((2, ROWS, TB), f32),
             pltpu.VMEM((2, ROWS, LANE), f32),
             pltpu.VMEM((NX + 1, 2, LANE, LANE), bf16),
-            pltpu.VMEM((NX + 2, 2, LANE, LANE), bf16),
+            pltpu.VMEM((2 * NX, 2, LANE, LANE), bf16),
             dma((NQ,)),
             dma((NQ,)),
             dma((NB,)),
@@ -746,7 +755,7 @@
             dma((2, NT)),
             dma((NB, NT)),
             dma((NX + 1, NT)),
-            dma((NX + 2, NT)),
+            dma((2 * NX, NT)),
         ],
         compiler_params=pltpu.CompilerParams(
             collective_id=0, has_side_effects=True, vmem_limit_bytes=56 * 1024 * 1024

time: 99.9 us -> 99.7 us (level)
  no operation moved by 1% of the time
where the time goes in v4:
time: 99.7 us; the launch traced here: 99.1 us
  Pallas kernels  95 us (95%)
  local copies, waits for them, and re-layouts  3.5 us (4%)
    pallas_call x1, Pallas kernels, per_device(): pl.pallas_call(kernel, out_shape=(out, out), in_specs=[pl.BlockSpec(memor...  95 us
    unnamed x4, local copies, waits for them, and re-layouts  3.5 us

profile of v4, /device:TPU:17, one launch (start us, length us, event | category | flops | bytes accessed | tf_op | source)
XLA Modules:
  0.0 99.1 jit_solution(2177598185461943423)
XLA Ops:
  0.6 95.0 %shard_map.41 = (f32[2,128,512]{2,1,0:T(8,128)}, f32[2,128,512]{2,1,0:T(8,128)}) custom-call(f32[8,128]{1,0:T(8,128)} %bitcast.9, bf16[1024,512]{1,0:T(8,128)(2,1)} %z_ref.1), custom_call_target="tpu_custom_call" | custom-call | tf_op jit(solution)/shard_map/pallas_call | solution.py:708
  95.6 0.0 copy-start
  95.6 2.3 %copy.4 = f32[1,128,2,512]{3,2,1,0:T(2,128)} copy(f32[1,128,2,512]{3,1,2,0:T(8,128)} %bitcast.8) | data formatting | bytes 1048576
  97.9 0.0 copy-done
  97.9 1.2 %copy.5 = f32[1,128,2,512]{3,2,1,0:T(2,128)} copy(f32[1,128,2,512]{3,1,2,0:T(8,128)S(1)} %bitcast.7) | data formatting | bytes 1048576
Async XLA Ops:
  95.6 2.3 %copy-start = (f32[2,128,512]{2,1,0:T(8,128)S(1)}, f32[2,128,512]{2,1,0:T(8,128)}, u32[]{:S(2)}) copy-start(f32[2,128,512]{2,1,0:T(8,128)} %get-tuple-element.5) | copy-start | bytes 1572868

commit v5 on v4

--- a/solution.py
+++ b/solution.py
@@ -274,7 +274,6 @@
     def _(k):
         g_copy(k).start()
 
-    send_chunk(1)
     allst[g] = stage[...]
     make_chunk(2)
     make_chunk(3)
@@ -340,7 +339,7 @@
     pltpu.make_async_copy(cbuf, cbuf, c_recv.at[1]).wait()
     weigh_columns(cbuf, other)
 
-    send_chunk(2)
+    send_chunk(1)
 
     def part_rows(t):
         return pl.ds(pl.multiple_of(t * PART, PART), PART)
@@ -497,13 +496,14 @@
         def _():
             pass_on(step + 1)
 
+        @pl.when(step < NT - 2)
+        def _():
+            send_chunk(step + 2)
+
         @pl.loop(0, W_STEP)
         def _(k):
             weight_sums(step * W_STEP + k)
 
-        @pl.when(step == 0)
-        def _():
-            send_chunk(NT - 1)
 
     @pl.loop(NT * W_STEP, NB)
     def _(b):

time: 99.7 us -> 95.4 us (0.957)
  Pallas kernels: 95 us -> 90.2 us
    pallas_call x1, Pallas kernels: 95 us -> 90.2 us  [per_device(): pl.pallas_call(kernel, out_shape=(out, out), in_specs=[pl.BlockSpec(memor...]
where the time goes in v5:
time: 95.4 us; the launch traced here: 94.3 us
  Pallas kernels  90.2 us (95%)
  local copies, waits for them, and re-layouts  3.5 us (4%)
    pallas_call x1, Pallas kernels, per_device(): pl.pallas_call(kernel, out_shape=(out, out), in_specs=[pl.BlockSpec(memor...  90.2 us
    unnamed x4, local copies, waits for them, and re-layouts  3.5 us

profile of v5, /device:TPU:17, one launch (start us, length us, event | category | flops | bytes accessed | tf_op | source)
XLA Modules:
  0.0 94.3 jit_solution(14040114632780449424)
XLA Ops:
  0.6 90.2 %shard_map.41 = (f32[2,128,512]{2,1,0:T(8,128)}, f32[2,128,512]{2,1,0:T(8,128)}) custom-call(f32[8,128]{1,0:T(8,128)} %bitcast.9, bf16[1024,512]{1,0:T(8,128)(2,1)} %z_ref.1), custom_call_target="tpu_custom_call" | custom-call | tf_op jit(solution)/shard_map/pallas_call | solution.py:708
  90.8 0.0 copy-start
  90.8 2.3 %copy.4 = f32[1,128,2,512]{3,2,1,0:T(2,128)} copy(f32[1,128,2,512]{3,1,2,0:T(8,128)} %bitcast.8) | data formatting | bytes 1048576
  93.1 0.0 copy-done
  93.1 1.2 %copy.5 = f32[1,128,2,512]{3,2,1,0:T(2,128)} copy(f32[1,128,2,512]{3,1,2,0:T(8,128)S(1)} %bitcast.7) | data formatting | bytes 1048576
Async XLA Ops:
  90.8 2.3 %copy-start = (f32[2,128,512]{2,1,0:T(8,128)S(1)}, f32[2,128,512]{2,1,0:T(8,128)}, u32[]{:S(2)}) copy-start(f32[2,128,512]{2,1,0:T(8,128)} %get-tuple-element.5) | copy-start | bytes 1572868

commit v6 on v5

--- a/solution.py
+++ b/solution.py
@@ -216,12 +216,16 @@
     core_copy(stage.at[y], stage.at[T_OTHER], 0).start()
     core_copy(z_ref, cbuf, 1).start()
 
-    def row_copy(way, c):
+    def half_of(q, c, h):
+        return rbuf.at[q, c, pl.ds(h * (SNP // 2), SNP // 2)]
+
+    def row_copy(way, c, p):
+        part = half_of(y, c, (way + p) % 2)
         return pltpu.make_async_remote_copy(
-            src_ref=rbuf.at[y, c],
-            dst_ref=rbuf.at[y, c],
-            send_sem=r_send.at[way, c],
-            recv_sem=r_recv.at[way, c],
+            src_ref=part,
+            dst_ref=part,
+            send_sem=r_send.at[way, p, c],
+            recv_sem=r_recv.at[way, p, c],
             device_id=(g, r, (y + 1 + 2 * way) % NQ),
             device_id_type=MESH,
         )
@@ -238,16 +242,16 @@
             device_id_type=MESH,
         )
 
-    def send_chunk(step):
-        row_copy(0, step).start()
-        row_copy(1, step).start()
+    def send_chunk(step, parts=(0, 1)):
+        for p in parts:
+            row_copy(0, step, p).start()
+            row_copy(1, step, p).start()
 
     def pass_on(step):
         for way in range(2):
             q = (y + 3 + 2 * way) % NQ
-            pltpu.make_async_copy(
-                rbuf.at[q, step], rbuf.at[q, step], r_recv.at[way, step]
-            ).wait()
+            part = half_of(q, step, way)
+            pltpu.make_async_copy(part, part, r_recv.at[way, 0, step]).wait()
             far_copy(way, step).start()
 
     send_chunk(0)
@@ -479,6 +483,8 @@
         for way in range(2):
             part = rbuf.at[far, step, pl.ds(way * (SNP // 2), SNP // 2)]
             pltpu.make_async_copy(part, part, f_recv.at[way, step]).wait()
+            part = half_of((y + 3 + 2 * way) % NQ, step, 1 - way)
+            pltpu.make_async_copy(part, part, r_recv.at[way, 1, step]).wait()
 
         @pl.loop(0, NQ)
         def _(k):
@@ -671,7 +677,8 @@
     @pl.loop(0, NX)
     def _(c):
         for way in range(2):
-            row_copy(way, c).wait_send()
+            row_copy(way, c, 0).wait_send()
+            row_copy(way, c, 1).wait_send()
             far_copy(way, c).wait_send()
 
     @pl.loop(1, NB)
@@ -746,8 +753,8 @@
             dma((NB,)),
             dma((2,)),
             dma((2,)),
-            dma((2, NT)),
-            dma((2, NT)),
+            dma((2, 2, NT)),
+            dma((2, 2, NT)),
             dma((2, NT)),
             dma((2, NT)),
             dma((NB, NT)),

time: 95.4 us -> 94.4 us (0.990)
  no operation moved by 1% of the time
where the time goes in v6:
time: 94.4 us; the launch traced here: 94.2 us
  Pallas kernels  90.1 us (95%)
  local copies, waits for them, and re-layouts  3.5 us (4%)
    pallas_call x1, Pallas kernels, per_device(): pl.pallas_call(kernel, out_shape=(out, out), in_specs=[pl.BlockSpec(memor...  90.1 us
    unnamed x4, local copies, waits for them, and re-layouts  3.5 us

profile of v6, /device:TPU:17, one launch (start us, length us, event | category | flops | bytes accessed | tf_op | source)
XLA Modules:
  0.0 94.2 jit_solution(1663930495955855237)
XLA Ops:
  0.6 90.1 %shard_map.41 = (f32[2,128,512]{2,1,0:T(8,128)}, f32[2,128,512]{2,1,0:T(8,128)}) custom-call(f32[8,128]{1,0:T(8,128)} %bitcast.9, bf16[1024,512]{1,0:T(8,128)(2,1)} %z_ref.1), custom_call_target="tpu_custom_call" | custom-call | tf_op jit(solution)/shard_map/pallas_call | solution.py:715
  90.7 0.0 copy-start
  90.7 2.3 %copy.4 = f32[1,128,2,512]{3,2,1,0:T(2,128)} copy(f32[1,128,2,512]{3,1,2,0:T(8,128)} %bitcast.8) | data formatting | bytes 1048576
  93.0 0.0 copy-done
  93.0 1.2 %copy.5 = f32[1,128,2,512]{3,2,1,0:T(2,128)} copy(f32[1,128,2,512]{3,1,2,0:T(8,128)S(1)} %bitcast.7) | data formatting | bytes 1048576
Async XLA Ops:
  90.7 2.3 %copy-start = (f32[2,128,512]{2,1,0:T(8,128)S(1)}, f32[2,128,512]{2,1,0:T(8,128)}, u32[]{:S(2)}) copy-start(f32[2,128,512]{2,1,0:T(8,128)} %get-tuple-element.5) | copy-start | bytes 1572868
